TPU v7x, 128 devices: a whole 4x4x4 slice. The times are simulated.
128 devices in a mesh: ctx: 16 (over y, z), head: 8 (over x, core).
Axes of the slice: x: 4, y: 4, z: 4, core: 2. Of those that a mesh axis runs over, the one named last changes fastest.
Arguments:
- queries: bfloat16 [8192, 5120], P('ctx', 'head'), may hold values from -6 to 6
- key_heads: bfloat16 [8192, 1024], P('ctx', 'head'), may hold values from -6 to 6
- value_heads: bfloat16 [8192, 1024], P('ctx', 'head'), may hold values from -24 to 24
- log_gates: float32 [8192, 8], P('ctx', 'head'), may hold values from -0.75 to 0, as said below
- norm_gain: float32 [5120], P('head'), may hold values from 0.25 to 1.75
- out_weight: bfloat16 [5120, 5120], P('head'), may hold values from -0.125 to 0.125
Outputs:
- layer_out: bfloat16 [5120, 8192], P('head', 'ctx')
Inputs may be any that keep to these rules, and one draw needn't show every extreme that they name: `log_gates`: every entry is negative.
All inputs are finite; a program needn't handle non-finite values.
Results may differ from a plain program's by a relative error of at most 0.017.
Values may be sent and summed in bfloat16 or wider, within the bound.
No kernel may reach another device: no remote copies, remote signals or barrier semaphores. Data moves between devices by JAX's collectives and lax.ppermute only.
A program may use at most 256 MiB of HBM per device.

v0:
```python
import jax
import jax.numpy as jnp
from jax import lax
from jax.experimental import pallas as pl
from jax.experimental.pallas import tpu as pltpu
from jax.sharding import PartitionSpec as P

HEAD_DIM = 128
GROUP_HEADS = 5
TOK = 512
PAY = TOK + 16
SIDE = 4
CHUNK = 640
BF = jnp.bfloat16
F32 = jnp.float32
VMEM = pl.BlockSpec(memory_space=pltpu.VMEM)

CTX = SIDE * SIDE
CTX_Z = {d: [(i, (i // SIDE) * SIDE + (i + d) % SIDE) for i in range(CTX)] for d in (1, -1)}
CTX_Y = {d: [(i, (i + d * SIDE) % CTX) for i in range(CTX)] for d in (1, -1, 2)}
HEAD_X = {d: [(i, (i + 2 * d) % (2 * SIDE)) for i in range(2 * SIDE)] for d in (1, -1)}
CORE = [(i, i ^ 1) for i in range(2 * SIDE)]


def kernel_call(body, outs, flops, nbytes, scratch=(), **extra):
    return pl.pallas_call(
        body,
        out_shape=outs,
        in_specs=extra.pop("in_specs"),
        out_specs=extra.pop("out_specs", jax.tree.map(lambda _: VMEM, outs)),
        scratch_shapes=list(scratch),
        compiler_params=pltpu.CompilerParams(vmem_limit_bytes=24 * 2**20),
        cost_estimate=pl.CostEstimate(flops=flops, bytes_accessed=nbytes, transcendentals=0),
        **extra,
    )


def shape(dims, kind):
    return jax.ShapeDtypeStruct(dims, kind)


def column(row):
    return jnp.broadcast_to(row, (HEAD_DIM, TOK)).T[:, :1]


def prepare_body(key_hbm, value_hbm, gate_hbm, out_ref, cum_ref, value_ref, gate_ref, sems):
    copies = [
        pltpu.make_async_copy(gate_hbm, gate_ref, sems.at[0]),
        pltpu.make_async_copy(value_hbm, value_ref, sems.at[1]),
        pltpu.make_async_copy(key_hbm, out_ref.at[pl.ds(0, TOK), pl.ds(0, HEAD_DIM)], sems.at[2]),
    ]
    for copy in copies:
        copy.start()
    copies[0].wait()
    gates = gate_ref[...]
    top = gates.astype(BF).astype(F32)
    mid = (gates - top).astype(BF).astype(F32)
    rows = lax.broadcasted_iota(jnp.int32, (16, TOK), 0)
    parts = jnp.where(rows == 0, top, jnp.where(rows == 1, mid, gates - top - mid))
    parts = jnp.where(rows < 3, parts, 0.0).astype(BF)
    source = lax.broadcasted_iota(jnp.int32, (TOK, TOK), 0)
    place = lax.broadcasted_iota(jnp.int32, (TOK, TOK), 1)
    upto = jnp.where(source <= place, 1.0, 0.0).astype(BF)
    sums = jnp.dot(parts, upto, preferred_element_type=F32)
    cum = jnp.sum(sums, axis=0, keepdims=True)
    cum_ref[...] = cum
    total = cum[:, TOK - 1 :]
    copies[1].wait()
    out_ref[:TOK, HEAD_DIM:] = (value_ref[...].astype(F32) * jnp.exp(total - column(cum))).astype(BF)
    top = total.astype(BF).astype(F32)
    mid = (total - top).astype(BF).astype(F32)
    rows = lax.broadcasted_iota(jnp.int32, (16, HEAD_DIM), 0)
    lanes = lax.broadcasted_iota(jnp.int32, (16, HEAD_DIM), 1)
    tile = jnp.where(lanes == 0, top, jnp.where(lanes == 1, mid, jnp.where(lanes == 2, total - top - mid, 0.0)))
    out_ref[TOK:, :HEAD_DIM] = jnp.where(rows == 0, tile, 0.0).astype(BF)
    out_ref[TOK:, HEAD_DIM:] = jnp.zeros((16, HEAD_DIM), BF)
    copies[2].wait()


def inner(query, key):
    return lax.dot_general(query, key, (((1,), (1,)), ((), ())), preferred_element_type=F32)


def head_cols(head):
    return slice(head * HEAD_DIM, (head + 1) * HEAD_DIM)


def own_body(query_ref, key_ref, value_ref, cum_ref, out_ref):
    cum_col = column(cum_ref[...])
    half = TOK // 2
    for part in range(2):
        rows = slice(part * half, (part + 1) * half)
        seen = (part + 1) * half
        place = part * half + lax.broadcasted_iota(jnp.int32, (half, seen), 0)
        source = lax.broadcasted_iota(jnp.int32, (half, seen), 1)
        decay = jnp.exp(jnp.minimum(cum_col[rows] - cum_ref[0:1, :seen], 0.0))
        decay = jnp.where(place >= source, decay, 0.0)
        for head in range(GROUP_HEADS):
            scores = inner(query_ref[rows, head_cols(head)], key_ref[:seen, :])
            scores = (scores * scores * decay).astype(BF)
            out_ref[rows, head_cols(head)] = jnp.dot(
                scores, value_ref[:seen, :], preferred_element_type=F32
            )


def total_of(ref, slot):
    tile = ref[slot * PAY + TOK : (slot + 1) * PAY, :HEAD_DIM].astype(F32)
    return jnp.sum(jnp.sum(tile, axis=1, keepdims=True), axis=0, keepdims=True)


def slot_places(place_z):
    return [place_z, (place_z + 3) % SIDE, (place_z + 1) % SIDE, (place_z + 2) % SIDE]


def gated(condition, value):
    return jnp.where(condition, value, jnp.zeros_like(value))


def later_sums(places, totals):
    return [
        sum(gated(places[i] > places[k], totals[i]) for i in range(SIDE) if i != k)
        for k in range(SIDE)
    ]


def stage(slot, log_decay, place, keys, values):
    ref, index = slot
    rows = slice(index * PAY, index * PAY + TOK)
    target = slice(place * TOK, (place + 1) * TOK)
    keys[target, :] = ref[rows, :HEAD_DIM]
    values[target, :] = (ref[rows, HEAD_DIM:].astype(F32) * jnp.exp(log_decay)).astype(BF)


def attend(query_ref, keys, values, start, size, acc_ref):
    rows = pl.ds(pl.multiple_of(start, size), size)
    key, value = keys[rows, :], values[rows, :]
    for head in range(GROUP_HEADS):
        scores = inner(query_ref[:, head_cols(head)], key)
        scores = (scores * scores).astype(BF)
        acc_ref[:, head_cols(head)] += jnp.dot(scores, value, preferred_element_type=F32)


def row_body(query_ref, own_ref, back_ref, ahead_ref, far_ref, acc_ref, stat_ref, keys, values):
    place_z = lax.axis_index("ctx") % SIDE
    places = slot_places(place_z)
    refs = [own_ref, back_ref, ahead_ref, far_ref]
    totals = [total_of(ref, 0) for ref in refs]
    acc_ref[...] = jnp.zeros_like(acc_ref)
    before = sum(gated(places[k] < place_z, totals[k]) for k in range(1, SIDE))
    stat_ref[...] = jnp.broadcast_to(before, stat_ref.shape)
    for k in range(1, SIDE):
        log_decay = sum(
            gated((places[i] > places[k]) & (places[i] < place_z), totals[i])
            for i in range(1, SIDE)
            if i != k
        )
        stage((refs[k], 0), log_decay, k - 1, keys, values)

    @pl.loop(0, SIDE - 1)
    def _(i):
        turn = jnp.where(i == 0, 3, i)
        is_before = (place_z + turn) % SIDE < place_z

        @pl.when(is_before)
        def _():
            attend(query_ref, keys, values, i * TOK, TOK, acc_ref)


def wanted(row):
    place_y = lax.axis_index("ctx") // SIDE
    return jnp.where(row == 0, place_y >= 1, place_y == SIDE - 1)


def first_body(query_ref, back_ref, ahead_ref, acc_ref, keys, values):
    zero = jnp.zeros((1, 1), F32)
    stage((back_ref, 0), zero, 0, keys, values)
    stage((ahead_ref, 0), zero, 1, keys, values)
    acc_ref[...] = jnp.zeros_like(acc_ref)

    @pl.loop(0, 2)
    def _(row):
        @pl.when(wanted(row))
        def _():
            attend(query_ref, keys, values, row * TOK, TOK, acc_ref.at[row])


def middle_body(query_ref, back0, back12, ahead0, ahead12, first_ref, acc_ref, keys, values):
    places = slot_places(lax.axis_index("ctx") % SIDE)
    later = [places[SIDE - 1] > places[k] for k in range(SIDE - 1)]
    for row, slots in enumerate(([(back0, 0), (back12, 0), (back12, 1)], [(ahead0, 0), (ahead12, 0), (ahead12, 1)])):
        totals = [total_of(*slot) for slot in slots]
        decays = [
            sum(gated(places[i] > places[k], totals[i]) for i in range(SIDE - 1) if i != k)
            for k in range(SIDE - 1)
        ]
        for k in (1, 2):
            stage(slots[k], decays[k], 2 * row + k - 1, keys, values)
        first = jnp.exp(decays[0]) * first_ref[row]
        acc_ref[row, 0] = gated(~later[0], first)
        acc_ref[row, 1] = gated(later[0], first)

    @pl.loop(0, 4)
    def _(i):
        row, slot = i // 2, 1 + i % 2
        group = jnp.where(slot == 1, later[1], later[2]).astype(jnp.int32)

        @pl.when(wanted(row))
        def _():
            attend(query_ref, keys, values, i * TOK, TOK, acc_ref.at[row, group])


def row_slots(first, middle, far):
    return [(first, 0), (middle, 0), (middle, 1), (far, 0)]


def near_body(
    query_ref, back0, back12, back3, ahead0, ahead12, ahead3, stat_ref, acc_in, groups,
    acc_ref, out_stat, keys, values
):
    places = slot_places(lax.axis_index("ctx") % SIDE)
    before = stat_ref[0:1, 0:1]
    for row, slots in enumerate((row_slots(back0, back12, back3), row_slots(ahead0, ahead12, ahead3))):
        totals = [total_of(*slot) for slot in slots]
        last = sum(gated(places[i] > places[SIDE - 1], totals[i]) for i in range(SIDE - 1))
        base = before if row == 0 else jnp.zeros_like(before)
        stage(slots[SIDE - 1], base + last, row, keys, values)
        both = jnp.exp(base) * groups[row, 0] + jnp.exp(base + totals[SIDE - 1]) * groups[row, 1]
        acc_ref[row] = acc_in[...] + both if row == 0 else both
        if row == 0:
            out_stat[...] = jnp.broadcast_to(before + sum(totals), out_stat.shape)

    @pl.loop(0, 2)
    def _(row):
        @pl.when(wanted(row))
        def _():
            attend(query_ref, keys, values, row * TOK, TOK, acc_ref.at[row])


def last_body(
    query_ref, far0, far12, far3, stat_ref, acc_in, own_ref, cum_ref, gain_ref,
    out_ref, acc, keys, values
):
    index = lax.axis_index("ctx")
    place_y, places = index // SIDE, slot_places(index % SIDE)
    before = stat_ref[0:1, 0:1]
    slots = row_slots(far0, far12, far3)
    totals = [total_of(*slot) for slot in slots]
    later = later_sums(places, totals)
    for k in range(SIDE):
        stage(slots[k], before + later[k], k, keys, values)
    acc[...] = acc_in[0]

    @pl.when(place_y == SIDE - 1)
    def _():
        acc[...] += jnp.exp(before + sum(totals)) * acc_in[1]

    @pl.when(place_y >= 2)
    def _():
        @pl.loop(0, 2)
        def _(i):
            attend(query_ref, keys, values, i * 2 * TOK, 2 * TOK, acc)

    grow = jnp.exp(column(cum_ref[...]))
    for head in range(GROUP_HEADS):
        cols = head_cols(head)
        number = own_ref[:, cols] + grow * acc[:, cols]
        mean = jnp.mean(number * number, axis=-1, keepdims=True)
        out_ref[:, cols] = (number * lax.rsqrt(mean + 1e-06) * gain_ref[0:1, cols]).astype(BF)


def features_of(weight_ref, step, flip):
    place = lax.axis_index("head")
    chunk = (place // 2 + step) % SIDE * 2 + (place % 2 + flip) % 2
    return weight_ref[:, pl.ds(pl.multiple_of(chunk * CHUNK, HEAD_DIM), CHUNK)]


def product(normed_ref, weight_ref, step, flip):
    return jnp.dot(
        normed_ref[...], features_of(weight_ref, step, flip), preferred_element_type=F32
    )


def other_far_body(normed_ref, weight_ref, out_ref):
    out_ref[...] = product(normed_ref, weight_ref, 2, 1).astype(BF)


def other_near_body(normed_ref, weight_ref, out_ref):
    @pl.loop(0, 3)
    def _(slot):
        step = jnp.where(slot == 0, 1, jnp.where(slot == 1, 3, 0))
        out_ref[slot] = product(normed_ref, weight_ref, step, 1).astype(BF)


def mine_far_body(normed_ref, weight_ref, other_ref, far_r, far_l):
    half = TOK // 2
    both = product(normed_ref, weight_ref, 2, 0) + other_ref[...].astype(F32)
    far_r[...] = both[:half].astype(BF)
    far_l[...] = both[half:].astype(BF)


def mine_near_body(normed_ref, weight_ref, other_ref, near_r, near_l, hold_r, hold_l, own_ref):
    half = TOK // 2
    both = product(normed_ref, weight_ref, 1, 0) + other_ref[0].astype(F32)
    hold_r[...] = both[:half]
    near_r[...] = both[half:].astype(BF)
    both = product(normed_ref, weight_ref, 3, 0) + other_ref[1].astype(F32)
    near_l[...] = both[:half].astype(BF)
    hold_l[...] = both[half:]
    own_ref[...] = product(normed_ref, weight_ref, 0, 0) + other_ref[2].astype(F32)


def pass_body(hold_r, far_r, hold_l, far_l, out_r, out_l):
    out_r[...] = (hold_r[...] + far_r[...].astype(F32)).astype(BF)
    out_l[...] = (hold_l[...] + far_l[...].astype(F32)).astype(BF)


def gather_body(own_ref, near_r, near_l, out_ref):
    half = TOK // 2
    out_ref[:half, :] = own_ref[:half, :] + near_l[...].astype(F32)
    out_ref[half:, :] = own_ref[half:, :] + near_r[...].astype(F32)


def finish_body(own_ref, sum_r, sum_l, out_ref):
    half = TOK // 2
    out_ref[:, :half] = (own_ref[:half, :] + sum_r[...].astype(F32)).T.astype(BF)
    out_ref[:, half:] = (own_ref[half:, :] + sum_l[...].astype(F32)).T.astype(BF)


def send(value, axis, pairs):
    return lax.ppermute(value, axis, pairs)


def per_device(queries, key_heads, value_heads, log_gates, norm_gain, out_weight):
    wide = GROUP_HEADS * HEAD_DIM
    after = lax.optimization_barrier
    payload, cum = kernel_call(
        prepare_body,
        (shape((PAY, 2 * HEAD_DIM), BF), shape((1, TOK), F32)),
        2**23,
        2**19,
        [pltpu.VMEM((TOK, HEAD_DIM), BF), pltpu.VMEM((1, TOK), F32), pltpu.SemaphoreType.DMA((3,))],
        in_specs=[pl.BlockSpec(memory_space=pltpu.HBM)] * 3,
    )(key_heads, value_heads, log_gates.reshape(1, TOK))
    row_back = send(payload, "ctx", CTX_Z[1])
    row_ahead = send(payload, "ctx", CTX_Z[-1])
    back0 = send(payload, "ctx", CTX_Y[1])
    ahead0 = send(payload, "ctx", CTX_Y[-1])
    block_flops = 4 * TOK * TOK * wide
    acc_shape, stat_shape = shape((TOK, wide), F32), shape((8, HEAD_DIM), F32)

    def scratch(blocks):
        return [pltpu.VMEM((blocks * TOK, HEAD_DIM), BF)] * 2

    own = kernel_call(own_body, acc_shape, block_flops, 2**21, in_specs=[VMEM] * 4)(
        queries, key_heads, value_heads, cum
    )
    row_far = send(row_back, "ctx", CTX_Z[1])
    middle = jnp.concatenate([row_back, row_ahead], axis=0)
    middle, own = after((middle, own))
    back12 = send(middle, "ctx", CTX_Y[1])
    ahead12 = send(middle, "ctx", CTX_Y[-1])
    first = kernel_call(
        first_body, shape((2, TOK, wide), F32), 2 * block_flops, 2**21, scratch(2), in_specs=[VMEM] * 3
    )(queries, back0, ahead0)
    acc, stat = kernel_call(
        row_body, (acc_shape, stat_shape), 3 * block_flops, 2**21, scratch(3), in_specs=[VMEM] * 5
    )(queries, payload, row_back, row_ahead, row_far)
    pass_back, pass_ahead, pass0, pass_far, acc, first = after(
        (back12, ahead12, ahead0, row_far, acc, first)
    )
    far12 = send(pass_back, "ctx", CTX_Y[1])
    far0 = send(pass0, "ctx", CTX_Y[-1])
    back3 = send(pass_back[PAY:], "ctx", CTX_Z[-1])
    ahead3 = send(pass_ahead[:PAY], "ctx", CTX_Z[1])
    far3 = send(pass_far, "ctx", CTX_Y[2])
    groups = kernel_call(
        middle_body,
        shape((2, 2, TOK, wide), F32),
        24 * block_flops,
        2**22,
        scratch(4),
        in_specs=[VMEM] * 6,
    )(queries, back0, back12, ahead0, ahead12, first)
    acc, stat = kernel_call(
        near_body,
        (shape((2, TOK, wide), F32), stat_shape),
        2 * block_flops,
        2**22,
        scratch(2),
        in_specs=[VMEM] * 10,
    )(queries, back0, back12, back3, ahead0, ahead12, ahead3, stat, acc, groups)
    normed = kernel_call(
        last_body,
        shape((TOK, wide), BF),
        4 * block_flops,
        2**22,
        [pltpu.VMEM((TOK, wide), F32), *scratch(4)],
        in_specs=[VMEM] * 9,
    )(queries, far0, far12, far3, stat, acc, own, cum, norm_gain.reshape(1, wide))

    chunk_flops = 2 * TOK * CHUNK * wide
    chunk = shape((TOK, CHUNK), BF)
    half_bf, half_f32 = shape((TOK // 2, CHUNK), BF), shape((TOK // 2, CHUNK), F32)
    other_far = kernel_call(other_far_body, chunk, chunk_flops, 2**20, in_specs=[VMEM] * 2)(
        normed, out_weight
    )
    normed, other_far = after((normed, other_far))
    other_far = send(other_far, "head", CORE)
    other_near = kernel_call(
        other_near_body, shape((3, TOK, CHUNK), BF), 30 * chunk_flops, 2**21, in_specs=[VMEM] * 2
    )(normed, out_weight)
    other_near = send(other_near, "head", CORE)
    far_r, far_l = kernel_call(
        mine_far_body, (half_bf, half_bf), 30 * chunk_flops, 2**20, in_specs=[VMEM] * 3
    )(normed, out_weight, other_far)
    far_r = send(far_r, "head", HEAD_X[1])
    far_l = send(far_l, "head", HEAD_X[-1])
    near_r, near_l, hold_r, hold_l, own_sum = kernel_call(
        mine_near_body,
        (half_bf, half_bf, half_f32, half_f32, shape((TOK, CHUNK), F32)),
        3 * chunk_flops,
        2**22,
        in_specs=[VMEM] * 3,
    )(normed, out_weight, other_near)
    near_r = send(near_r, "head", HEAD_X[1])
    near_l = send(near_l, "head", HEAD_X[-1])
    sum_r, sum_l = kernel_call(pass_body, (half_bf,) * 2, 2**19, 2**21, in_specs=[VMEM] * 4)(
        hold_r, far_r, hold_l, far_l
    )
    sum_r = send(sum_r, "head", HEAD_X[1])
    sum_l = send(sum_l, "head", HEAD_X[-1])
    own_sum = kernel_call(
        gather_body, shape((TOK, CHUNK), F32), 2**20, 2**22, in_specs=[VMEM] * 3
    )(own_sum, near_r, near_l)
    return kernel_call(finish_body, shape((CHUNK, TOK), BF), 2**20, 2**22, in_specs=[VMEM] * 3)(
        own_sum, sum_r, sum_l
    )


def solution(mesh):
    return jax.shard_map(
        per_device,
        mesh=mesh,
        in_specs=(
            P("ctx", "head"),
            P("ctx", "head"),
            P("ctx", "head"),
            P("ctx", "head"),
            P("head"),
            P("head", None),
        ),
        out_specs=P("head", "ctx"),
        check_vma=False,
    )
```

profile of v0, /device:TPU:30, one launch (start us, length us, event | category | flops | bytes accessed | tf_op | source)
XLA Modules:
  0.0 85.0 jit_solution(15348231007004278401)
XLA Ops:
  0.0 0.0 copy-start.2
  0.0 0.9 %copy-done.2 = bf16[512,128]{1,0:T(8,128)(2,1)S(1)} copy-done((bf16[512,128]{1,0:T(8,128)(2,1)S(1)}, bf16[512,128]{1,0:T(8,128)(2,1)}, u32[]{:S(2)}) %copy-start.2) | copy-done | bytes 131096
  0.9 0.9 %copy-done.3 = bf16[512,128]{1,0:T(8,128)(2,1)S(1)} copy-done((bf16[512,128]{1,0:T(8,128)(2,1)S(1)}, bf16[512,128]{1,0:T(8,128)(2,1)}, u32[]{:S(2)}) %copy-start.3) | copy-done | bytes 131096
  1.8 0.7 copy-done.4
  2.5 0.7 shard_map.64
  3.2 2.0 %collective-permute-start = (bf16[528,256]{1,0:T(8,128)(2,1)S(1)}, bf16[528,256]{1,0:T(8,128)(2,1)S(1)}, u32[]{:S(2)}, u32[]{:S(2)}) collective-permute-start(bf16[528,256]{1,0:T(8,128)(2,1)S(1)} %get-tuple-element.30.own_ref), channel_id=1, source_target_pairs={{0,8},{8,16},{16,24},{24,0},{32,40},{40,48},{48,56},{56,32},{64,72... | collective-permute-start | bytes 811016 | tf_op jit(solution)/shard_map/ppermute | solution.py:330
  5.2 2.2 %collective-permute-start.1 = (bf16[528,256]{1,0:T(8,128)(2,1)S(1)}, bf16[528,256]{1,0:T(8,128)(2,1)S(1)}, u32[]{:S(2)}, u32[]{:S(2)}) collective-permute-start(bf16[528,256]{1,0:T(8,128)(2,1)S(1)} %get-tuple-element.30.own_ref), channel_id=1, source_target_pairs={{0,24},{8,0},{16,8},{24,16},{32,56},{40,32},{48,40},{56,48},{64,88... | collective-permute-start | bytes 811016 | tf_op jit(solution)/shard_map/ppermute | solution.py:330
  7.4 0.7 collective-permute-start.4
  8.1 2.5 %collective-permute-start.6 = (bf16[528,256]{1,0:T(8,128)(2,1)S(1)}, bf16[528,256]{1,0:T(8,128)(2,1)S(1)}, u32[]{:S(2)}, u32[]{:S(2)}) collective-permute-start(bf16[528,256]{1,0:T(8,128)(2,1)S(1)} %get-tuple-element.30.own_ref), channel_id=1, source_target_pairs={{0,32},{8,40},{16,48},{24,56},{32,64},{40,72},{48,80},{56,88},{64,... | collective-permute-start | bytes 811016 | tf_op jit(solution)/shard_map/ppermute | solution.py:330
  10.6 1.1 %copy-done = bf16[512,640]{1,0:T(8,128)(2,1)S(1)} copy-done((bf16[512,640]{1,0:T(8,128)(2,1)S(1)}, bf16[512,640]{1,0:T(8,128)(2,1)}, u32[]{:S(2)}) %copy-start) | copy-done | bytes 655384
  11.7 1.8 %shard_map.65.own_ref = f32[512,640]{1,0:T(8,128)S(1)} custom-call(bf16[512,640]{1,0:T(8,128)(2,1)S(1)} %copy-done, bf16[512,128]{1,0:T(8,128)(2,1)S(1)} %copy-done.2, bf16[512,128]{1,0:T(8,128)(2,1)S(1)} %copy-done.3, f32[1,512]{1,0:T(1,128)S(1)} %get-tuple-element.31.cum_ref), custom_call_target="tpu_custom_call" | custom-call | flops 671088640 | bytes 2097152 | tf_op jit(solution)/shard_map/pallas_call | solution.py:354
  13.5 0.3 collective-permute-done.back_ref
  13.8 0.0 collective-permute-done.1.ahead_ref
  13.8 0.3 collective-permute-start.2
  14.1 1.8 %collective-permute-start.3 = (bf16[1056,256]{1,0:T(8,128)(2,1)S(1)}, bf16[1056,256]{1,0:T(8,128)(2,1)S(1)}, u32[]{:S(2)}, u32[]{:S(2)}) collective-permute-start(bf16[1056,256]{1,0:T(8,128)(2,1)S(1)} %pad_maximum_fusion), channel_id=1, source_target_pairs={{0,96},{8,104},{16,112},{24,120},{32,0},{40,8},{48,16},{56,24},{64... | collective-permute-start | bytes 1622024 | tf_op jit(solution)/shard_map/ppermute | solution.py:330
  15.9 1.3 %collective-permute-start.5 = (bf16[528,256]{1,0:T(8,128)(2,1)S(1)}, bf16[528,256]{1,0:T(8,128)(2,1)S(1)}, u32[]{:S(2)}, u32[]{:S(2)}) collective-permute-start(bf16[528,256]{1,0:T(8,128)(2,1)S(1)} %collective-permute-done.back_ref), channel_id=1, source_target_pairs={{0,8},{8,16},{16,24},{24,0},{32,40},{40,48},{48,56},{56,32},{64,72... | collective-permute-start | bytes 811016 | tf_op jit(solution)/shard_map/ppermute | solution.py:330
  17.2 0.0 copy-done.5
  17.2 0.0 collective-permute-done.4.ahead_ref.ahead0
  17.2 0.4 collective-permute-done.6.back_ref.back0
  17.6 0.0 copy-done.1
  17.6 3.4 %shard_map.67.first_ref = f32[2,512,640]{2,1,0:T(8,128)S(1)} custom-call(bf16[512,640]{1,0:T(8,128)(2,1)S(1)} %copy-done.1, bf16[528,256]{1,0:T(8,128)(2,1)S(1)} %collective-permute-done.6.back_ref.back0, bf16[528,256]{1,0:T(8,128)(2,1)S(1)} %collective-permute-done.4.ahead_ref.ahead0), custom_call_target="tpu_custom_call" | custom-call | flops 1342177280 | bytes 2097152 | tf_op jit(solution)/shard_map/pallas_call | solution.py:362
  20.9 3.3 %collective-permute-done.5.far_ref = bf16[528,256]{1,0:T(8,128)(2,1)S(1)} collective-permute-done((bf16[528,256]{1,0:T(8,128)(2,1)S(1)}, bf16[528,256]{1,0:T(8,128)(2,1)S(1)}, u32[]{:S(2)}, u32[]{:S(2)}) %collective-permute-start.5) | collective-permute-done | bytes 270368 | tf_op jit(solution)/shard_map/ppermute | solution.py:330
  24.2 0.3 shard_map.66
  24.5 2.8 %collective-permute-done.2.back12 = bf16[1056,256]{1,0:T(8,128)(2,1)S(1)} collective-permute-done((bf16[1056,256]{1,0:T(8,128)(2,1)S(1)}, bf16[1056,256]{1,0:T(8,128)(2,1)S(1)}, u32[]{:S(2)}, u32[]{:S(2)}) %collective-permute-start.2) | collective-permute-done | bytes 540704 | tf_op jit(solution)/shard_map/ppermute | solution.py:330
  27.4 1.3 %collective-permute-done.3.ahead12 = bf16[1056,256]{1,0:T(8,128)(2,1)S(1)} collective-permute-done((bf16[1056,256]{1,0:T(8,128)(2,1)S(1)}, bf16[1056,256]{1,0:T(8,128)(2,1)S(1)}, u32[]{:S(2)}, u32[]{:S(2)}) %collective-permute-start.3) | collective-permute-done | bytes 540704 | tf_op jit(solution)/shard_map/ppermute | solution.py:330
  28.7 2.5 %collective-permute-start.8 = (bf16[1056,256]{1,0:T(8,128)(2,1)S(1)}, bf16[1056,256]{1,0:T(8,128)(2,1)S(1)}, u32[]{:S(2)}, u32[]{:S(2)}) collective-permute-start(bf16[1056,256]{1,0:T(8,128)(2,1)S(1)} %collective-permute-done.2.back12), channel_id=1, source_target_pairs={{0,32},{8,40},{16,48},{24,56},{32,64},{40,72},{48,80},{56,88},{64,... | collective-permute-start | bytes 1622024 | tf_op jit(solution)/shard_map/ppermute | solution.py:330
  31.2 1.7 %collective-permute-start.10 = (bf16[528,256]{1,0:T(8,128)(2,1)S(1)}, bf16[528,256]{1,0:T(8,128)(2,1)S(1)}, u32[]{:S(2)}, u32[]{:S(2)}) collective-permute-start(bf16[528,256]{1,0:T(8,128)(2,1)S(1)} %slice.6), channel_id=1, source_target_pairs={{0,24},{8,0},{16,8},{24,16},{32,56},{40,32},{48,40},{56,48},{64,88... | collective-permute-start | bytes 811016 | tf_op jit(solution)/shard_map/ppermute | solution.py:330
  32.9 0.4 collective-permute-start.11
  33.3 0.4 collective-permute-start.7
  33.7 1.2 %collective-permute-start.9 = (bf16[528,256]{1,0:T(8,128)(2,1)S(1)}, bf16[528,256]{1,0:T(8,128)(2,1)S(1)}, u32[]{:S(2)}, u32[]{:S(2)}) collective-permute-start(bf16[528,256]{1,0:T(8,128)(2,1)S(1)} %collective-permute-done.5.far_ref), channel_id=1, source_target_pairs={{0,64},{8,72},{16,80},{24,88},{32,96},{40,104},{48,112},{56,120},{... | collective-permute-start | bytes 811016 | tf_op jit(solution)/shard_map/ppermute | solution.py:330
  34.9 6.9 %shard_map.68.groups = f32[2,2,512,640]{3,2,1,0:T(8,128)S(1)} custom-call(bf16[512,640]{1,0:T(8,128)(2,1)S(1)} %copy-done.1, bf16[528,256]{1,0:T(8,128)(2,1)S(1)} %collective-permute-done.6.back_ref.back0, bf16[1056,256]{1,0:T(8,128)(2,1)S(1)} %collective-permute-done.2.back12, bf16[528,256]{1,0:T(8,128)(2,1)S(1)} %collective-permute-done.4.ahead_ref.ahead0, ...), custom_call_target="tpu_custom_call" | custom-call | flops 16106127360 | bytes 4194304 | tf_op jit(solution)/shard_map/pallas_call | solution.py:376
  41.8 0.0 collective-permute-done.10.back3
  41.8 0.0 collective-permute-done.11.ahead3
  41.9 0.0 slice-start
  41.9 3.9 %shard_map.69 = (f32[2,512,640]{2,1,0:T(8,128)S(1)}, f32[8,128]{1,0:T(8,128)S(1)}) custom-call(bf16[512,640]{1,0:T(8,128)(2,1)S(1)} %copy-done.1, bf16[528,256]{1,0:T(8,128)(2,1)S(1)} %collective-permute-done.6.back_ref.back0, bf16[1056,256]{1,0:T(8,128)(2,1)S(1)} %collective-permute-done.2.back12, bf16[528,256]{1,0:T(8,128)(2,1)S(1)} %collective-permute-done.10.back3, ...), custom_call_target="tpu_custom_call" | custom-call | flops 1342177280 | bytes 4194304 | tf_op jit(solution)/shard_map/pallas_call | solution.py:384
  45.8 1.0 %collective-permute-done.7.far0 = bf16[528,256]{1,0:T(8,128)(2,1)S(1)} collective-permute-done((bf16[528,256]{1,0:T(8,128)(2,1)S(1)}, bf16[528,256]{1,0:T(8,128)(2,1)S(1)}, u32[]{:S(2)}, u32[]{:S(2)}) %collective-permute-start.7) | collective-permute-done | bytes 270368 | tf_op jit(solution)/shard_map/ppermute | solution.py:330
  46.8 0.0 collective-permute-done.9.far3
  46.8 0.2 collective-permute-done.8.far12
  47.1 7.0 %shard_map.70.normed_ref = bf16[512,640]{1,0:T(8,128)(2,1)S(1)} custom-call(bf16[512,640]{1,0:T(8,128)(2,1)S(1)} %copy-done.1, bf16[528,256]{1,0:T(8,128)(2,1)S(1)} %collective-permute-done.7.far0, bf16[1056,256]{1,0:T(8,128)(2,1)S(1)} %collective-permute-done.8.far12, bf16[528,256]{1,0:T(8,128)(2,1)S(1)} %collective-permute-done.9.far3, ...), custom_call_target="tpu_custom_call" | custom-call | flops 2684354560 | bytes 4194304 | tf_op jit(solution)/shard_map/pallas_call | solution.py:392
  54.0 0.0 slice-done
  54.0 0.0 slice-done.1
  54.1 0.8 shard_map.71
  54.8 0.1 collective-permute-start.15
  54.9 2.3 %shard_map.72 = bf16[3,512,640]{2,1,0:T(8,128)(2,1)S(1)} custom-call(bf16[512,640]{1,0:T(8,128)(2,1)S(1)} %shard_map.70.normed_ref, bf16[640,5120]{1,0:T(8,128)(2,1)S(1)} %bitcast.2), custom_call_target="tpu_custom_call" | custom-call | flops 12582912000 | bytes 2097152 | tf_op jit(solution)/shard_map/pallas_call | solution.py:409
  57.3 0.5 collective-permute-start.12
  57.8 0.0 collective-permute-done.15.other_ref
  57.8 0.8 shard_map.75
  58.6 0.5 collective-permute-start.16
  59.2 1.5 %collective-permute-start.17 = (bf16[256,640]{1,0:T(8,128)(2,1)S(1)}, bf16[256,640]{1,0:T(8,128)(2,1)S(1)}, u32[]{:S(2)}, u32[]{:S(2)}) collective-permute-start(bf16[256,640]{1,0:T(8,128)(2,1)S(1)} %get-tuple-element.52), channel_id=1, source_target_pairs={{0,6},{1,7},{2,0},{3,1},{4,2},{5,3},{6,4},{7,5},{8,14},{9,15},{10,... | collective-permute-start | bytes 983048 | tf_op jit(solution)/shard_map/ppermute | solution.py:330
  60.7 0.7 collective-permute-done.12.other_ref
  61.4 2.0 %shard_map.73 = (bf16[256,640]{1,0:T(8,128)(2,1)S(1)}, bf16[256,640]{1,0:T(8,128)(2,1)S(1)}, f32[256,640]{1,0:T(8,128)S(1)}, f32[256,640]{1,0:T(8,128)S(1)}, f32[512,640]{1,0:T(8,128)S(1)}) custom-call(bf16[512,640]{1,0:T(8,128)(2,1)S(1)} %shard_map.70.normed_ref, bf16[640,5120]{1,0:T(8,128)(2,1)S(1)} %bitcast.2, ...), custom_call_target="tpu_custom_call" | custom-call | flops 1258291200 | bytes 4194304 | tf_op jit(solution)/shard_map/pallas_call | solution.py:418
  63.4 1.0 %collective-permute-start.13 = (bf16[256,640]{1,0:T(8,128)(2,1)S(1)}, bf16[256,640]{1,0:T(8,128)(2,1)S(1)}, u32[]{:S(2)}, u32[]{:S(2)}) collective-permute-start(bf16[256,640]{1,0:T(8,128)(2,1)S(1)} %get-tuple-element.46), channel_id=1, source_target_pairs={{0,2},{1,3},{2,4},{3,5},{4,6},{5,7},{6,0},{7,1},{8,10},{9,11},{10,... | collective-permute-start | bytes 983048 | tf_op jit(solution)/shard_map/ppermute | solution.py:330
  64.4 1.1 %collective-permute-start.14 = (bf16[256,640]{1,0:T(8,128)(2,1)S(1)}, bf16[256,640]{1,0:T(8,128)(2,1)S(1)}, u32[]{:S(2)}, u32[]{:S(2)}) collective-permute-start(bf16[256,640]{1,0:T(8,128)(2,1)S(1)} %get-tuple-element.47), channel_id=1, source_target_pairs={{0,6},{1,7},{2,0},{3,1},{4,2},{5,3},{6,4},{7,5},{8,14},{9,15},{10,... | collective-permute-start | bytes 983048 | tf_op jit(solution)/shard_map/ppermute | solution.py:330
  65.5 3.7 %collective-permute-done.16.far_r = bf16[256,640]{1,0:T(8,128)(2,1)S(1)} collective-permute-done((bf16[256,640]{1,0:T(8,128)(2,1)S(1)}, bf16[256,640]{1,0:T(8,128)(2,1)S(1)}, u32[]{:S(2)}, u32[]{:S(2)}) %collective-permute-start.16) | collective-permute-done | bytes 327712 | tf_op jit(solution)/shard_map/ppermute | solution.py:330
  69.2 1.7 %collective-permute-done.17.far_l = bf16[256,640]{1,0:T(8,128)(2,1)S(1)} collective-permute-done((bf16[256,640]{1,0:T(8,128)(2,1)S(1)}, bf16[256,640]{1,0:T(8,128)(2,1)S(1)}, u32[]{:S(2)}, u32[]{:S(2)}) %collective-permute-start.17) | collective-permute-done | bytes 327712 | tf_op jit(solution)/shard_map/ppermute | solution.py:330
  71.0 0.1 shard_map.76
  71.1 0.4 collective-permute-start.18
  71.5 1.7 %collective-permute-start.19 = (bf16[256,640]{1,0:T(8,128)(2,1)S(1)}, bf16[256,640]{1,0:T(8,128)(2,1)S(1)}, u32[]{:S(2)}, u32[]{:S(2)}) collective-permute-start(bf16[256,640]{1,0:T(8,128)(2,1)S(1)} %get-tuple-element.54), channel_id=1, source_target_pairs={{0,6},{1,7},{2,0},{3,1},{4,2},{5,3},{6,4},{7,5},{8,14},{9,15},{10,... | collective-permute-start | bytes 983048 | tf_op jit(solution)/shard_map/ppermute | solution.py:330
  73.2 3.1 %collective-permute-done.13.near_r = bf16[256,640]{1,0:T(8,128)(2,1)S(1)} collective-permute-done((bf16[256,640]{1,0:T(8,128)(2,1)S(1)}, bf16[256,640]{1,0:T(8,128)(2,1)S(1)}, u32[]{:S(2)}, u32[]{:S(2)}) %collective-permute-start.13) | collective-permute-done | bytes 327712 | tf_op jit(solution)/shard_map/ppermute | solution.py:330
  76.3 1.7 %collective-permute-done.14.near_l = bf16[256,640]{1,0:T(8,128)(2,1)S(1)} collective-permute-done((bf16[256,640]{1,0:T(8,128)(2,1)S(1)}, bf16[256,640]{1,0:T(8,128)(2,1)S(1)}, u32[]{:S(2)}, u32[]{:S(2)}) %collective-permute-start.14) | collective-permute-done | bytes 327712 | tf_op jit(solution)/shard_map/ppermute | solution.py:330
  78.0 0.1 shard_map.74.own_ref
  78.1 4.3 %collective-permute-done.18.sum_r = bf16[256,640]{1,0:T(8,128)(2,1)S(1)} collective-permute-done((bf16[256,640]{1,0:T(8,128)(2,1)S(1)}, bf16[256,640]{1,0:T(8,128)(2,1)S(1)}, u32[]{:S(2)}, u32[]{:S(2)}) %collective-permute-start.18) | collective-permute-done | bytes 327712 | tf_op jit(solution)/shard_map/ppermute | solution.py:330
  82.4 1.5 %collective-permute-done.19.sum_l = bf16[256,640]{1,0:T(8,128)(2,1)S(1)} collective-permute-done((bf16[256,640]{1,0:T(8,128)(2,1)S(1)}, bf16[256,640]{1,0:T(8,128)(2,1)S(1)}, u32[]{:S(2)}, u32[]{:S(2)}) %collective-permute-start.19) | collective-permute-done | bytes 327712 | tf_op jit(solution)/shard_map/ppermute | solution.py:330
  83.9 1.1 %shard_map.77 = bf16[640,512]{1,0:T(8,128)(2,1)} custom-call(f32[512,640]{1,0:T(8,128)S(1)} %shard_map.74.own_ref, bf16[256,640]{1,0:T(8,128)(2,1)S(1)} %collective-permute-done.18.sum_r, bf16[256,640]{1,0:T(8,128)(2,1)S(1)} %collective-permute-done.19.sum_l), custom_call_target="tpu_custom_call" | custom-call | flops 1048576 | bytes 4194304 | tf_op jit(solution)/shard_map/pallas_call | solution.py:435
  (11 shorter events, 0.1 us)
Async XLA Ops:
  0.0 0.9 %copy-start.2 = (bf16[512,128]{1,0:T(8,128)(2,1)S(1)}, bf16[512,128]{1,0:T(8,128)(2,1)}, u32[]{:S(2)}) copy-start(bf16[512,128]{1,0:T(8,128)(2,1)} %key_ref.1) | copy-start | bytes 393220
  0.9 0.9 %copy-start.3 = (bf16[512,128]{1,0:T(8,128)(2,1)S(1)}, bf16[512,128]{1,0:T(8,128)(2,1)}, u32[]{:S(2)}) copy-start(bf16[512,128]{1,0:T(8,128)(2,1)} %value_ref.1) | copy-start | bytes 393220
  1.8 0.7 copy-start.4
  3.2 10.6 %collective-permute-start = (bf16[528,256]{1,0:T(8,128)(2,1)S(1)}, bf16[528,256]{1,0:T(8,128)(2,1)S(1)}, u32[]{:S(2)}, u32[]{:S(2)}) collective-permute-start(bf16[528,256]{1,0:T(8,128)(2,1)S(1)} %get-tuple-element.30.own_ref), channel_id=1, source_target_pairs={{0,8},{8,16},{16,24},{24,0},{32,40},{40,48},{48,56},{56,32},{64,72... | collective-permute-start | bytes 811016 | tf_op jit(solution)/shard_map/ppermute | solution.py:330
  5.2 8.6 %collective-permute-start.1 = (bf16[528,256]{1,0:T(8,128)(2,1)S(1)}, bf16[528,256]{1,0:T(8,128)(2,1)S(1)}, u32[]{:S(2)}, u32[]{:S(2)}) collective-permute-start(bf16[528,256]{1,0:T(8,128)(2,1)S(1)} %get-tuple-element.30.own_ref), channel_id=1, source_target_pairs={{0,24},{8,0},{16,8},{24,16},{32,56},{40,32},{48,40},{56,48},{64,88... | collective-permute-start | bytes 811016 | tf_op jit(solution)/shard_map/ppermute | solution.py:330
  7.4 9.8 %collective-permute-start.4 = (bf16[528,256]{1,0:T(8,128)(2,1)S(1)}, bf16[528,256]{1,0:T(8,128)(2,1)S(1)}, u32[]{:S(2)}, u32[]{:S(2)}) collective-permute-start(bf16[528,256]{1,0:T(8,128)(2,1)S(1)} %get-tuple-element.30.own_ref), channel_id=1, source_target_pairs={{0,96},{8,104},{16,112},{24,120},{32,0},{40,8},{48,16},{56,24},{64... | collective-permute-start | bytes 811016 | tf_op jit(solution)/shard_map/ppermute | solution.py:330
  8.1 9.4 %collective-permute-start.6 = (bf16[528,256]{1,0:T(8,128)(2,1)S(1)}, bf16[528,256]{1,0:T(8,128)(2,1)S(1)}, u32[]{:S(2)}, u32[]{:S(2)}) collective-permute-start(bf16[528,256]{1,0:T(8,128)(2,1)S(1)} %get-tuple-element.30.own_ref), channel_id=1, source_target_pairs={{0,32},{8,40},{16,48},{24,56},{32,64},{40,72},{48,80},{56,88},{64,... | collective-permute-start | bytes 811016 | tf_op jit(solution)/shard_map/ppermute | solution.py:330
  10.6 1.1 %copy-start = (bf16[512,640]{1,0:T(8,128)(2,1)S(1)}, bf16[512,640]{1,0:T(8,128)(2,1)}, u32[]{:S(2)}) copy-start(bf16[512,640]{1,0:T(8,128)(2,1)} %query_ref.11) | copy-start | bytes 1966084
  11.7 5.5 %copy-start.5 = (f32[640]{0:T(1024)S(1)}, f32[640]{0:T(1024)}, u32[]{:S(2)}) copy-start(f32[640]{0:T(1024)} %param.10) | copy-start | bytes 7684
  11.7 5.9 %copy-start.1 = (bf16[512,640]{1,0:T(8,128)(2,1)S(1)}, bf16[512,640]{1,0:T(8,128)(2,1)}, u32[]{:S(2)}) copy-start(bf16[512,640]{1,0:T(8,128)(2,1)} %query_ref.11) | copy-start | bytes 1966084
  13.8 13.6 %collective-permute-start.2 = (bf16[1056,256]{1,0:T(8,128)(2,1)S(1)}, bf16[1056,256]{1,0:T(8,128)(2,1)S(1)}, u32[]{:S(2)}, u32[]{:S(2)}) collective-permute-start(bf16[1056,256]{1,0:T(8,128)(2,1)S(1)} %pad_maximum_fusion), channel_id=1, source_target_pairs={{0,32},{8,40},{16,48},{24,56},{32,64},{40,72},{48,80},{56,88},{64,... | collective-permute-start | bytes 1622024 | tf_op jit(solution)/shard_map/ppermute | solution.py:330
  14.1 14.5 %collective-permute-start.3 = (bf16[1056,256]{1,0:T(8,128)(2,1)S(1)}, bf16[1056,256]{1,0:T(8,128)(2,1)S(1)}, u32[]{:S(2)}, u32[]{:S(2)}) collective-permute-start(bf16[1056,256]{1,0:T(8,128)(2,1)S(1)} %pad_maximum_fusion), channel_id=1, source_target_pairs={{0,96},{8,104},{16,112},{24,120},{32,0},{40,8},{48,16},{56,24},{64... | collective-permute-start | bytes 1622024 | tf_op jit(solution)/shard_map/ppermute | solution.py:330
  15.9 8.3 %collective-permute-start.5 = (bf16[528,256]{1,0:T(8,128)(2,1)S(1)}, bf16[528,256]{1,0:T(8,128)(2,1)S(1)}, u32[]{:S(2)}, u32[]{:S(2)}) collective-permute-start(bf16[528,256]{1,0:T(8,128)(2,1)S(1)} %collective-permute-done.back_ref), channel_id=1, source_target_pairs={{0,8},{8,16},{16,24},{24,0},{32,40},{40,48},{48,56},{56,32},{64,72... | collective-permute-start | bytes 811016 | tf_op jit(solution)/shard_map/ppermute | solution.py:330
  28.7 18.4 %collective-permute-start.8 = (bf16[1056,256]{1,0:T(8,128)(2,1)S(1)}, bf16[1056,256]{1,0:T(8,128)(2,1)S(1)}, u32[]{:S(2)}, u32[]{:S(2)}) collective-permute-start(bf16[1056,256]{1,0:T(8,128)(2,1)S(1)} %collective-permute-done.2.back12), channel_id=1, source_target_pairs={{0,32},{8,40},{16,48},{24,56},{32,64},{40,72},{48,80},{56,88},{64,... | collective-permute-start | bytes 1622024 | tf_op jit(solution)/shard_map/ppermute | solution.py:330
  31.2 10.7 %collective-permute-start.10 = (bf16[528,256]{1,0:T(8,128)(2,1)S(1)}, bf16[528,256]{1,0:T(8,128)(2,1)S(1)}, u32[]{:S(2)}, u32[]{:S(2)}) collective-permute-start(bf16[528,256]{1,0:T(8,128)(2,1)S(1)} %slice.6), channel_id=1, source_target_pairs={{0,24},{8,0},{16,8},{24,16},{32,56},{40,32},{48,40},{56,48},{64,88... | collective-permute-start | bytes 811016 | tf_op jit(solution)/shard_map/ppermute | solution.py:330
  32.9 9.0 %collective-permute-start.11 = (bf16[528,256]{1,0:T(8,128)(2,1)S(1)}, bf16[528,256]{1,0:T(8,128)(2,1)S(1)}, u32[]{:S(2)}, u32[]{:S(2)}) collective-permute-start(bf16[528,256]{1,0:T(8,128)(2,1)S(1)} %slice.7), channel_id=1, source_target_pairs={{0,8},{8,16},{16,24},{24,0},{32,40},{40,48},{48,56},{56,32},{64,72... | collective-permute-start | bytes 811016 | tf_op jit(solution)/shard_map/ppermute | solution.py:330
  33.3 13.5 %collective-permute-start.7 = (bf16[528,256]{1,0:T(8,128)(2,1)S(1)}, bf16[528,256]{1,0:T(8,128)(2,1)S(1)}, u32[]{:S(2)}, u32[]{:S(2)}) collective-permute-start(bf16[528,256]{1,0:T(8,128)(2,1)S(1)} %collective-permute-done.4.ahead_ref.ahead0), channel_id=1, source_target_pairs={{0,96},{8,104},{16,112},{24,120},{32,0},{40,8},{48,16},{56,24},{64... | collective-permute-start | bytes 811016 | tf_op jit(solution)/shard_map/ppermute | solution.py:330
  33.7 13.2 %collective-permute-start.9 = (bf16[528,256]{1,0:T(8,128)(2,1)S(1)}, bf16[528,256]{1,0:T(8,128)(2,1)S(1)}, u32[]{:S(2)}, u32[]{:S(2)}) collective-permute-start(bf16[528,256]{1,0:T(8,128)(2,1)S(1)} %collective-permute-done.5.far_ref), channel_id=1, source_target_pairs={{0,64},{8,72},{16,80},{24,88},{32,96},{40,104},{48,112},{56,120},{... | collective-permute-start | bytes 811016 | tf_op jit(solution)/shard_map/ppermute | solution.py:330
  41.9 12.2 %slice-start = ((s8[6553600]{0:T(1024)(128)(4,1)}), s8[4194304]{0:T(1024)(128)(4,1)S(1)}, s32[]{:S(2)}) async-start(s8[6553600]{0:T(1024)(128)(4,1)} %bitcast.1), calls=%async_computation | async-start | bytes 8388608
  47.1 7.0 %slice-start.1 = ((s8[6553600]{0:T(1024)(128)(4,1)}), s8[2359296]{0:T(1024)(128)(4,1)S(1)}, s32[]{:S(2)}) async-start(s8[6553600]{0:T(1024)(128)(4,1)} %bitcast.1), calls=%async_computation.1 | async-start | bytes 4718592
  54.8 3.0 %collective-permute-start.15 = (bf16[512,640]{1,0:T(8,128)(2,1)S(1)}, bf16[512,640]{1,0:T(8,128)(2,1)S(1)}, u32[]{:S(2)}, u32[]{:S(2)}) collective-permute-start(bf16[512,640]{1,0:T(8,128)(2,1)S(1)} %shard_map.71), channel_id=1, source_target_pairs={{0,1},{1,0},{2,3},{3,2},{4,5},{5,4},{6,7},{7,6},{8,9},{9,8},{10,11... | collective-permute-start | bytes 1966088 | tf_op jit(solution)/shard_map/ppermute | solution.py:330
  57.3 4.1 %collective-permute-start.12 = (bf16[3,512,640]{2,1,0:T(8,128)(2,1)S(1)}, bf16[3,512,640]{2,1,0:T(8,128)(2,1)S(1)}, u32[]{:S(2)}, u32[]{:S(2)}) collective-permute-start(bf16[3,512,640]{2,1,0:T(8,128)(2,1)S(1)} %shard_map.72), channel_id=1, source_target_pairs={{0,1},{1,0},{2,3},{3,2},{4,5},{5,4},{6,7},{7,6},{8,9},{9,8},{10,11... | collective-permute-start | bytes 5898248 | tf_op jit(solution)/shard_map/ppermute | solution.py:330
  58.6 10.6 %collective-permute-start.16 = (bf16[256,640]{1,0:T(8,128)(2,1)S(1)}, bf16[256,640]{1,0:T(8,128)(2,1)S(1)}, u32[]{:S(2)}, u32[]{:S(2)}) collective-permute-start(bf16[256,640]{1,0:T(8,128)(2,1)S(1)} %get-tuple-element.50), channel_id=1, source_target_pairs={{0,2},{1,3},{2,4},{3,5},{4,6},{5,7},{6,0},{7,1},{8,10},{9,11},{10,... | collective-permute-start | bytes 983048 | tf_op jit(solution)/shard_map/ppermute | solution.py:330
  59.2 11.8 %collective-permute-start.17 = (bf16[256,640]{1,0:T(8,128)(2,1)S(1)}, bf16[256,640]{1,0:T(8,128)(2,1)S(1)}, u32[]{:S(2)}, u32[]{:S(2)}) collective-permute-start(bf16[256,640]{1,0:T(8,128)(2,1)S(1)} %get-tuple-element.52), channel_id=1, source_target_pairs={{0,6},{1,7},{2,0},{3,1},{4,2},{5,3},{6,4},{7,5},{8,14},{9,15},{10,... | collective-permute-start | bytes 983048 | tf_op jit(solution)/shard_map/ppermute | solution.py:330
  63.4 12.9 %collective-permute-start.13 = (bf16[256,640]{1,0:T(8,128)(2,1)S(1)}, bf16[256,640]{1,0:T(8,128)(2,1)S(1)}, u32[]{:S(2)}, u32[]{:S(2)}) collective-permute-start(bf16[256,640]{1,0:T(8,128)(2,1)S(1)} %get-tuple-element.46), channel_id=1, source_target_pairs={{0,2},{1,3},{2,4},{3,5},{4,6},{5,7},{6,0},{7,1},{8,10},{9,11},{10,... | collective-permute-start | bytes 983048 | tf_op jit(solution)/shard_map/ppermute | solution.py:330
  64.4 13.6 %collective-permute-start.14 = (bf16[256,640]{1,0:T(8,128)(2,1)S(1)}, bf16[256,640]{1,0:T(8,128)(2,1)S(1)}, u32[]{:S(2)}, u32[]{:S(2)}) collective-permute-start(bf16[256,640]{1,0:T(8,128)(2,1)S(1)} %get-tuple-element.47), channel_id=1, source_target_pairs={{0,6},{1,7},{2,0},{3,1},{4,2},{5,3},{6,4},{7,5},{8,14},{9,15},{10,... | collective-permute-start | bytes 983048 | tf_op jit(solution)/shard_map/ppermute | solution.py:330
  71.1 11.3 %collective-permute-start.18 = (bf16[256,640]{1,0:T(8,128)(2,1)S(1)}, bf16[256,640]{1,0:T(8,128)(2,1)S(1)}, u32[]{:S(2)}, u32[]{:S(2)}) collective-permute-start(bf16[256,640]{1,0:T(8,128)(2,1)S(1)} %get-tuple-element.53), channel_id=1, source_target_pairs={{0,2},{1,3},{2,4},{3,5},{4,6},{5,7},{6,0},{7,1},{8,10},{9,11},{10,... | collective-permute-start | bytes 983048 | tf_op jit(solution)/shard_map/ppermute | solution.py:330
  71.5 12.4 %collective-permute-start.19 = (bf16[256,640]{1,0:T(8,128)(2,1)S(1)}, bf16[256,640]{1,0:T(8,128)(2,1)S(1)}, u32[]{:S(2)}, u32[]{:S(2)}) collective-permute-start(bf16[256,640]{1,0:T(8,128)(2,1)S(1)} %get-tuple-element.54), channel_id=1, source_target_pairs={{0,6},{1,7},{2,0},{3,1},{4,2},{5,3},{6,4},{7,5},{8,14},{9,15},{10,... | collective-permute-start | bytes 983048 | tf_op jit(solution)/shard_map/ppermute | solution.py:330
where the time goes:
time: 85.8 us; the launch traced here: 85 us
  Pallas kernels  31.1 us (36%)
  waiting for transfers between devices  26.1 us (30%)
  starting transfers between devices  23.9 us (28%)
  local copies, waits for them, and re-layouts  3.63 us (4%)
    ppermute x20, waiting for transfers between devices, send(): return lax.ppermute(value, axis, pairs)  26.1 us
    ppermute x20, starting transfers between devices, send(): return lax.ppermute(value, axis, pairs)  23.9 us
    pallas_call x1, Pallas kernels, per_device(): kernel_call(last_body, shape((TOK, wide), BF), 4 * block_flops, 2 ** 22,...  6.96 us
    pallas_call x1, Pallas kernels, per_device(): kernel_call(middle_body, shape((2, 2, TOK, wide), F32), 24 * block_flops,...  6.93 us
    pallas_call x1, Pallas kernels, per_device(): kernel_call(near_body, (shape((2, TOK, wide), F32), stat_shape), 2 * bloc...  3.93 us
    unnamed x16, local copies, waits for them, and re-layouts  3.59 us
    pallas_call x1, Pallas kernels, per_device(): kernel_call(first_body, shape((2, TOK, wide), F32), 2 * block_flops, 2 **...  3.36 us
    pallas_call x1, Pallas kernels, per_device(): kernel_call(other_near_body, shape((3, TOK, CHUNK), BF), 30 * chunk_flops...  2.35 us
  transfers between devices with their start and end apart: 20, of which 14 were waited for; matrix products, arithmetic and copies ran while one was open for 0% of the time, Pallas kernels for 25%

commit v1 on v0

--- a/solution.py
+++ b/solution.py
@@ -22,14 +22,14 @@
 CORE = [(i, i ^ 1) for i in range(2 * SIDE)]
 
 
-def kernel_call(body, outs, flops, nbytes, scratch=(), **extra):
+def kernel_call(body, outs, flops, nbytes, scratch=(), vmem=24 * 2**20, **extra):
     return pl.pallas_call(
         body,
         out_shape=outs,
         in_specs=extra.pop("in_specs"),
         out_specs=extra.pop("out_specs", jax.tree.map(lambda _: VMEM, outs)),
         scratch_shapes=list(scratch),
-        compiler_params=pltpu.CompilerParams(vmem_limit_bytes=24 * 2**20),
+        compiler_params=pltpu.CompilerParams(vmem_limit_bytes=vmem),
         cost_estimate=pl.CostEstimate(flops=flops, bytes_accessed=nbytes, transcendentals=0),
         **extra,
     )
@@ -339,6 +339,7 @@
         2**23,
         2**19,
         [pltpu.VMEM((TOK, HEAD_DIM), BF), pltpu.VMEM((1, TOK), F32), pltpu.SemaphoreType.DMA((3,))],
+        vmem=60 * 2**20,
         in_specs=[pl.BlockSpec(memory_space=pltpu.HBM)] * 3,
     )(key_heads, value_heads, log_gates.reshape(1, TOK))
     row_back = send(payload, "ctx", CTX_Z[1])
@@ -351,28 +352,28 @@
     def scratch(blocks):
         return [pltpu.VMEM((blocks * TOK, HEAD_DIM), BF)] * 2
 
-    own = kernel_call(own_body, acc_shape, block_flops, 2**21, in_specs=[VMEM] * 4)(
-        queries, key_heads, value_heads, cum
-    )
     row_far = send(row_back, "ctx", CTX_Z[1])
     middle = jnp.concatenate([row_back, row_ahead], axis=0)
-    middle, own = after((middle, own))
+    middle, own_keys = after((middle, key_heads))
+    own = kernel_call(own_body, acc_shape, 8 * block_flops, 2**21, in_specs=[VMEM] * 4)(
+        queries, own_keys, value_heads, cum
+    )
+    first0, own = after((back0, own))
     back12 = send(middle, "ctx", CTX_Y[1])
     ahead12 = send(middle, "ctx", CTX_Y[-1])
     first = kernel_call(
         first_body, shape((2, TOK, wide), F32), 2 * block_flops, 2**21, scratch(2), in_specs=[VMEM] * 3
-    )(queries, back0, ahead0)
+    )(queries, first0, ahead0)
+    pass0, row_far, first = after((ahead0, row_far, first))
+    far0 = send(pass0, "ctx", CTX_Y[-1])
     acc, stat = kernel_call(
-        row_body, (acc_shape, stat_shape), 3 * block_flops, 2**21, scratch(3), in_specs=[VMEM] * 5
+        row_body, (acc_shape, stat_shape), 24 * block_flops, 2**21, scratch(3), in_specs=[VMEM] * 5
     )(queries, payload, row_back, row_ahead, row_far)
-    pass_back, pass_ahead, pass0, pass_far, acc, first = after(
-        (back12, ahead12, ahead0, row_far, acc, first)
-    )
+    pass_back, pass_far, acc = after((back12, row_far, acc))
     far12 = send(pass_back, "ctx", CTX_Y[1])
-    far0 = send(pass0, "ctx", CTX_Y[-1])
     back3 = send(pass_back[PAY:], "ctx", CTX_Z[-1])
-    ahead3 = send(pass_ahead[:PAY], "ctx", CTX_Z[1])
     far3 = send(pass_far, "ctx", CTX_Y[2])
+    ahead3 = send(ahead12[:PAY], "ctx", CTX_Z[1])
     groups = kernel_call(
         middle_body,
         shape((2, 2, TOK, wide), F32),

time: 85.8 us -> 82.9 us (0.966)
  local copies, waits for them, and re-layouts: 3.63 us -> 1.44 us
  waiting for transfers between devices: 26.1 us -> 24.3 us
  Pallas kernels: 31.1 us -> 32.5 us
    unnamed x16, local copies, waits for them, and re-layouts: 3.59 us -> 0.72 us
    ppermute x20, waiting for transfers between devices: 26.1 us -> 24.3 us  [send(): return lax.ppermute(value, axis, pairs)]
    pallas_call x1, Pallas kernels: 0.7 us -> 2.04 us  [per_device(): kernel_call(prepare_body, (shape((PAY, 2 * HEAD_DIM), BF), shape((1, TOK)...]
  transfers between devices with their start and end apart: 20 -> 20, of which waited for: 14 -> 11; matrix products, arithmetic and copies ran while one was open for 0% -> 1% of each run, Pallas kernels for 25% -> 26%
where the time goes in v1:
time: 82.9 us; the launch traced here: 82.7 us
  Pallas kernels  32.5 us (39%)
  waiting for transfers between devices  24.3 us (29%)
  starting transfers between devices  24.2 us (29%)
  local copies, waits for them, and re-layouts  1.44 us (2%)
    ppermute x20, waiting for transfers between devices, send(): return lax.ppermute(value, axis, pairs)  24.3 us
    ppermute x20, starting transfers between devices, send(): return lax.ppermute(value, axis, pairs)  24.2 us
    pallas_call x1, Pallas kernels, per_device(): kernel_call(last_body, shape((TOK, wide), BF), 4 * block_flops, 2 ** 22,...  6.97 us
    pallas_call x1, Pallas kernels, per_device(): kernel_call(middle_body, shape((2, 2, TOK, wide), F32), 24 * block_flops,...  6.93 us
    pallas_call x1, Pallas kernels, per_device(): kernel_call(near_body, (shape((2, TOK, wide), F32), stat_shape), 2 * bloc...  3.91 us
    pallas_call x1, Pallas kernels, per_device(): kernel_call(first_body, shape((2, TOK, wide), F32), 2 * block_flops, 2 **...  3.38 us
    pallas_call x1, Pallas kernels, per_device(): kernel_call(other_near_body, shape((3, TOK, CHUNK), BF), 30 * chunk_flops...  2.34 us
    pallas_call x1, Pallas kernels, per_device(): kernel_call(prepare_body, (shape((PAY, 2 * HEAD_DIM), BF), shape((1, TOK)...  2.04 us
  transfers between devices with their start and end apart: 20, of which 11 were waited for; matrix products, arithmetic and copies ran while one was open for 1% of the time, Pallas kernels for 26%

profile of v1, /device:TPU:30, one launch (start us, length us, event | category | flops | bytes accessed | tf_op | source)
XLA Modules:
  0.0 82.7 jit_solution(5573877606669043349)
XLA Ops:
  0.0 2.0 %shard_map.64 = (bf16[528,256]{1,0:T(8,128)(2,1)}, f32[1,512]{1,0:T(1,128)}) custom-call(bf16[512,128]{1,0:T(8,128)(2,1)} %key_ref, bf16[512,128]{1,0:T(8,128)(2,1)} %value_ref.1, f32[1,512]{1,0:T(1,128)} %bitcast.3), custom_call_target="tpu_custom_call" | custom-call | flops 8388608 | bytes 524288 | tf_op jit(solution)/shard_map/pallas_call | solution.py:336
  2.1 2.0 %collective-permute-start.1 = (bf16[528,256]{1,0:T(8,128)(2,1)}, bf16[528,256]{1,0:T(8,128)(2,1)S(1)}, u32[]{:S(2)}, u32[]{:S(2)}) collective-permute-start(bf16[528,256]{1,0:T(8,128)(2,1)} %get-tuple-element.32.own_ref), channel_id=1, source_target_pairs={{0,8},{8,16},{16,24},{24,0},{32,40},{40,48},{48,56},{56,32},{64,72... | collective-permute-start | bytes 811016 | tf_op jit(solution)/shard_map/ppermute | solution.py:330
  4.0 2.2 %collective-permute-start.4 = (bf16[528,256]{1,0:T(8,128)(2,1)}, bf16[528,256]{1,0:T(8,128)(2,1)S(1)}, u32[]{:S(2)}, u32[]{:S(2)}) collective-permute-start(bf16[528,256]{1,0:T(8,128)(2,1)} %get-tuple-element.32.own_ref), channel_id=1, source_target_pairs={{0,24},{8,0},{16,8},{24,16},{32,56},{40,32},{48,40},{56,48},{64,88... | collective-permute-start | bytes 811016 | tf_op jit(solution)/shard_map/ppermute | solution.py:330
  6.2 0.2 collective-permute-start.3
  6.5 1.8 %collective-permute-start = (bf16[528,256]{1,0:T(8,128)(2,1)}, bf16[528,256]{1,0:T(8,128)(2,1)S(1)}, u32[]{:S(2)}, u32[]{:S(2)}) collective-permute-start(bf16[528,256]{1,0:T(8,128)(2,1)} %get-tuple-element.32.own_ref), channel_id=1, source_target_pairs={{0,96},{8,104},{16,112},{24,120},{32,0},{40,8},{48,16},{56,24},{64... | collective-permute-start | bytes 811016 | tf_op jit(solution)/shard_map/ppermute | solution.py:330
  8.3 0.7 reshape.7.gain_ref
  9.0 3.9 %collective-permute-done.1.back_ref = bf16[528,256]{1,0:T(8,128)(2,1)S(1)} collective-permute-done((bf16[528,256]{1,0:T(8,128)(2,1)}, bf16[528,256]{1,0:T(8,128)(2,1)S(1)}, u32[]{:S(2)}, u32[]{:S(2)}) %collective-permute-start.1) | collective-permute-done | bytes 270368 | tf_op jit(solution)/shard_map/ppermute | solution.py:330
  12.9 0.0 collective-permute-done.4.ahead_ref
  12.9 0.3 collective-permute-start.6
  13.2 1.8 %collective-permute-start.10 = (bf16[1056,256]{1,0:T(8,128)(2,1)S(1)}, bf16[1056,256]{1,0:T(8,128)(2,1)S(1)}, u32[]{:S(2)}, u32[]{:S(2)}) collective-permute-start(bf16[1056,256]{1,0:T(8,128)(2,1)S(1)} %pad_maximum_fusion), channel_id=1, source_target_pairs={{0,96},{8,104},{16,112},{24,120},{32,0},{40,8},{48,16},{56,24},{64... | collective-permute-start | bytes 1622024 | tf_op jit(solution)/shard_map/ppermute | solution.py:330
  15.0 1.3 %collective-permute-start.2 = (bf16[528,256]{1,0:T(8,128)(2,1)S(1)}, bf16[528,256]{1,0:T(8,128)(2,1)S(1)}, u32[]{:S(2)}, u32[]{:S(2)}) collective-permute-start(bf16[528,256]{1,0:T(8,128)(2,1)S(1)} %collective-permute-done.1.back_ref), channel_id=1, source_target_pairs={{0,8},{8,16},{16,24},{24,0},{32,40},{40,48},{48,56},{56,32},{64,72... | collective-permute-start | bytes 811016 | tf_op jit(solution)/shard_map/ppermute | solution.py:330
  16.2 0.0 copy-done.1
  16.3 0.0 copy-done.2
  16.3 0.0 copy-done
  16.3 0.7 copy-done.4
  16.9 1.8 %shard_map.65.own_ref = f32[512,640]{1,0:T(8,128)S(1)} custom-call(bf16[512,640]{1,0:T(8,128)(2,1)S(1)} %copy-done, bf16[512,128]{1,0:T(8,128)(2,1)S(1)} %copy-done.1, bf16[512,128]{1,0:T(8,128)(2,1)S(1)} %copy-done.2, f32[1,512]{1,0:T(1,128)S(1)} %copy-done.4), custom_call_target="tpu_custom_call" | custom-call | flops 5368709120 | bytes 2097152 | tf_op jit(solution)/shard_map/pallas_call | solution.py:358
  18.7 0.0 copy-start.3
  18.7 0.0 collective-permute-done.3.back_ref.back0
  18.8 0.0 collective-permute-done.ahead_ref.ahead0
  18.8 3.4 %shard_map.66.first_ref = f32[2,512,640]{2,1,0:T(8,128)S(1)} custom-call(bf16[512,640]{1,0:T(8,128)(2,1)S(1)} %copy-done, bf16[528,256]{1,0:T(8,128)(2,1)S(1)} %collective-permute-done.3.back_ref.back0, bf16[528,256]{1,0:T(8,128)(2,1)S(1)} %collective-permute-done.ahead_ref.ahead0), custom_call_target="tpu_custom_call" | custom-call | flops 1342177280 | bytes 2097152 | tf_op jit(solution)/shard_map/pallas_call | solution.py:364
  22.1 1.2 %collective-permute-done.2.far_ref = bf16[528,256]{1,0:T(8,128)(2,1)S(1)} collective-permute-done((bf16[528,256]{1,0:T(8,128)(2,1)S(1)}, bf16[528,256]{1,0:T(8,128)(2,1)S(1)}, u32[]{:S(2)}, u32[]{:S(2)}) %collective-permute-start.2) | collective-permute-done | bytes 270368 | tf_op jit(solution)/shard_map/ppermute | solution.py:330
  23.3 0.7 collective-permute-start.5
  24.1 0.3 shard_map.67
  24.4 2.1 %collective-permute-done.6.back12 = bf16[1056,256]{1,0:T(8,128)(2,1)S(1)} collective-permute-done((bf16[1056,256]{1,0:T(8,128)(2,1)S(1)}, bf16[1056,256]{1,0:T(8,128)(2,1)S(1)}, u32[]{:S(2)}, u32[]{:S(2)}) %collective-permute-start.6) | collective-permute-done | bytes 540704 | tf_op jit(solution)/shard_map/ppermute | solution.py:330
  26.5 1.6 %collective-permute-start.7 = (bf16[1056,256]{1,0:T(8,128)(2,1)S(1)}, bf16[1056,256]{1,0:T(8,128)(2,1)S(1)}, u32[]{:S(2)}, u32[]{:S(2)}) collective-permute-start(bf16[1056,256]{1,0:T(8,128)(2,1)S(1)} %collective-permute-done.6.back12), channel_id=1, source_target_pairs={{0,32},{8,40},{16,48},{24,56},{32,64},{40,72},{48,80},{56,88},{64,... | collective-permute-start | bytes 1622024 | tf_op jit(solution)/shard_map/ppermute | solution.py:330
  28.0 5.0 %collective-permute-start.9 = (bf16[528,256]{1,0:T(8,128)(2,1)S(1)}, bf16[528,256]{1,0:T(8,128)(2,1)S(1)}, u32[]{:S(2)}, u32[]{:S(2)}) collective-permute-start(bf16[528,256]{1,0:T(8,128)(2,1)S(1)} %slice.6), channel_id=1, source_target_pairs={{0,24},{8,0},{16,8},{24,16},{32,56},{40,32},{48,40},{56,48},{64,88... | collective-permute-start | bytes 811016 | tf_op jit(solution)/shard_map/ppermute | solution.py:330
  33.0 0.0 collective-permute-done.10.ahead12
  33.1 0.1 collective-permute-start.11
  33.1 0.3 collective-permute-start.8
  33.4 6.9 %shard_map.68.groups = f32[2,2,512,640]{3,2,1,0:T(8,128)S(1)} custom-call(bf16[512,640]{1,0:T(8,128)(2,1)S(1)} %copy-done, bf16[528,256]{1,0:T(8,128)(2,1)S(1)} %collective-permute-done.3.back_ref.back0, bf16[1056,256]{1,0:T(8,128)(2,1)S(1)} %collective-permute-done.6.back12, bf16[528,256]{1,0:T(8,128)(2,1)S(1)} %collective-permute-done.ahead_ref.ahead0, ...), custom_call_target="tpu_custom_call" | custom-call | flops 16106127360 | bytes 4194304 | tf_op jit(solution)/shard_map/pallas_call | solution.py:377
  40.4 0.0 collective-permute-done.9.back3
  40.4 0.4 collective-permute-done.11.ahead3
  40.8 3.9 %shard_map.69 = (f32[2,512,640]{2,1,0:T(8,128)S(1)}, f32[8,128]{1,0:T(8,128)S(1)}) custom-call(bf16[512,640]{1,0:T(8,128)(2,1)S(1)} %copy-done, bf16[528,256]{1,0:T(8,128)(2,1)S(1)} %collective-permute-done.3.back_ref.back0, bf16[1056,256]{1,0:T(8,128)(2,1)S(1)} %collective-permute-done.6.back12, bf16[528,256]{1,0:T(8,128)(2,1)S(1)} %collective-permute-done.9.back3, ...), custom_call_target="tpu_custom_call" | custom-call | flops 1342177280 | bytes 4194304 | tf_op jit(solution)/shard_map/pallas_call | solution.py:385
  44.7 0.0 collective-permute-done.5.far0
  44.7 0.0 collective-permute-done.8.far3
  44.7 0.0 collective-permute-done.7.far12
  44.8 0.0 copy-done.5
  44.8 0.0 slice-start.1
  44.8 7.0 %shard_map.70.normed_ref = bf16[512,640]{1,0:T(8,128)(2,1)S(1)} custom-call(bf16[512,640]{1,0:T(8,128)(2,1)S(1)} %copy-done, bf16[528,256]{1,0:T(8,128)(2,1)S(1)} %collective-permute-done.5.far0, bf16[1056,256]{1,0:T(8,128)(2,1)S(1)} %collective-permute-done.7.far12, bf16[528,256]{1,0:T(8,128)(2,1)S(1)} %collective-permute-done.8.far3, ...), custom_call_target="tpu_custom_call" | custom-call | flops 2684354560 | bytes 4194304 | tf_op jit(solution)/shard_map/pallas_call | solution.py:393
  51.8 0.0 slice-done
  51.8 0.0 slice-done.1
  51.8 0.8 shard_map.71
  52.6 0.1 collective-permute-start.15
  52.7 2.3 %shard_map.72 = bf16[3,512,640]{2,1,0:T(8,128)(2,1)S(1)} custom-call(bf16[512,640]{1,0:T(8,128)(2,1)S(1)} %shard_map.70.normed_ref, bf16[640,5120]{1,0:T(8,128)(2,1)S(1)} %bitcast.2), custom_call_target="tpu_custom_call" | custom-call | flops 12582912000 | bytes 2097152 | tf_op jit(solution)/shard_map/pallas_call | solution.py:410
  55.0 0.5 collective-permute-start.12
  55.6 0.0 collective-permute-done.15.other_ref
  55.6 0.8 shard_map.75
  56.3 0.5 collective-permute-start.16
  56.9 1.6 %collective-permute-start.17 = (bf16[256,640]{1,0:T(8,128)(2,1)S(1)}, bf16[256,640]{1,0:T(8,128)(2,1)S(1)}, u32[]{:S(2)}, u32[]{:S(2)}) collective-permute-start(bf16[256,640]{1,0:T(8,128)(2,1)S(1)} %get-tuple-element.56), channel_id=1, source_target_pairs={{0,6},{1,7},{2,0},{3,1},{4,2},{5,3},{6,4},{7,5},{8,14},{9,15},{10,... | collective-permute-start | bytes 983048 | tf_op jit(solution)/shard_map/ppermute | solution.py:330
  58.4 0.7 collective-permute-done.12.other_ref
  59.2 2.0 %shard_map.73 = (bf16[256,640]{1,0:T(8,128)(2,1)S(1)}, bf16[256,640]{1,0:T(8,128)(2,1)S(1)}, f32[256,640]{1,0:T(8,128)S(1)}, f32[256,640]{1,0:T(8,128)S(1)}, f32[512,640]{1,0:T(8,128)S(1)}) custom-call(bf16[512,640]{1,0:T(8,128)(2,1)S(1)} %shard_map.70.normed_ref, bf16[640,5120]{1,0:T(8,128)(2,1)S(1)} %bitcast.2, ...), custom_call_target="tpu_custom_call" | custom-call | flops 1258291200 | bytes 4194304 | tf_op jit(solution)/shard_map/pallas_call | solution.py:419
  61.1 1.0 %collective-permute-start.13 = (bf16[256,640]{1,0:T(8,128)(2,1)S(1)}, bf16[256,640]{1,0:T(8,128)(2,1)S(1)}, u32[]{:S(2)}, u32[]{:S(2)}) collective-permute-start(bf16[256,640]{1,0:T(8,128)(2,1)S(1)} %get-tuple-element.50), channel_id=1, source_target_pairs={{0,2},{1,3},{2,4},{3,5},{4,6},{5,7},{6,0},{7,1},{8,10},{9,11},{10,... | collective-permute-start | bytes 983048 | tf_op jit(solution)/shard_map/ppermute | solution.py:330
  62.2 1.1 %collective-permute-start.14 = (bf16[256,640]{1,0:T(8,128)(2,1)S(1)}, bf16[256,640]{1,0:T(8,128)(2,1)S(1)}, u32[]{:S(2)}, u32[]{:S(2)}) collective-permute-start(bf16[256,640]{1,0:T(8,128)(2,1)S(1)} %get-tuple-element.51), channel_id=1, source_target_pairs={{0,6},{1,7},{2,0},{3,1},{4,2},{5,3},{6,4},{7,5},{8,14},{9,15},{10,... | collective-permute-start | bytes 983048 | tf_op jit(solution)/shard_map/ppermute | solution.py:330
  63.2 3.7 %collective-permute-done.16.far_r = bf16[256,640]{1,0:T(8,128)(2,1)S(1)} collective-permute-done((bf16[256,640]{1,0:T(8,128)(2,1)S(1)}, bf16[256,640]{1,0:T(8,128)(2,1)S(1)}, u32[]{:S(2)}, u32[]{:S(2)}) %collective-permute-start.16) | collective-permute-done | bytes 327712 | tf_op jit(solution)/shard_map/ppermute | solution.py:330
  67.0 1.7 %collective-permute-done.17.far_l = bf16[256,640]{1,0:T(8,128)(2,1)S(1)} collective-permute-done((bf16[256,640]{1,0:T(8,128)(2,1)S(1)}, bf16[256,640]{1,0:T(8,128)(2,1)S(1)}, u32[]{:S(2)}, u32[]{:S(2)}) %collective-permute-start.17) | collective-permute-done | bytes 327712 | tf_op jit(solution)/shard_map/ppermute | solution.py:330
  68.7 0.1 shard_map.76
  68.8 0.4 collective-permute-start.18
  69.2 1.7 %collective-permute-start.19 = (bf16[256,640]{1,0:T(8,128)(2,1)S(1)}, bf16[256,640]{1,0:T(8,128)(2,1)S(1)}, u32[]{:S(2)}, u32[]{:S(2)}) collective-permute-start(bf16[256,640]{1,0:T(8,128)(2,1)S(1)} %get-tuple-element.58), channel_id=1, source_target_pairs={{0,6},{1,7},{2,0},{3,1},{4,2},{5,3},{6,4},{7,5},{8,14},{9,15},{10,... | collective-permute-start | bytes 983048 | tf_op jit(solution)/shard_map/ppermute | solution.py:330
  70.9 3.1 %collective-permute-done.13.near_r = bf16[256,640]{1,0:T(8,128)(2,1)S(1)} collective-permute-done((bf16[256,640]{1,0:T(8,128)(2,1)S(1)}, bf16[256,640]{1,0:T(8,128)(2,1)S(1)}, u32[]{:S(2)}, u32[]{:S(2)}) %collective-permute-start.13) | collective-permute-done | bytes 327712 | tf_op jit(solution)/shard_map/ppermute | solution.py:330
  74.0 1.7 %collective-permute-done.14.near_l = bf16[256,640]{1,0:T(8,128)(2,1)S(1)} collective-permute-done((bf16[256,640]{1,0:T(8,128)(2,1)S(1)}, bf16[256,640]{1,0:T(8,128)(2,1)S(1)}, u32[]{:S(2)}, u32[]{:S(2)}) %collective-permute-start.14) | collective-permute-done | bytes 327712 | tf_op jit(solution)/shard_map/ppermute | solution.py:330
  75.7 0.1 shard_map.74.own_ref
  75.8 4.3 %collective-permute-done.18.sum_r = bf16[256,640]{1,0:T(8,128)(2,1)S(1)} collective-permute-done((bf16[256,640]{1,0:T(8,128)(2,1)S(1)}, bf16[256,640]{1,0:T(8,128)(2,1)S(1)}, u32[]{:S(2)}, u32[]{:S(2)}) %collective-permute-start.18) | collective-permute-done | bytes 327712 | tf_op jit(solution)/shard_map/ppermute | solution.py:330
  80.1 1.5 %collective-permute-done.19.sum_l = bf16[256,640]{1,0:T(8,128)(2,1)S(1)} collective-permute-done((bf16[256,640]{1,0:T(8,128)(2,1)S(1)}, bf16[256,640]{1,0:T(8,128)(2,1)S(1)}, u32[]{:S(2)}, u32[]{:S(2)}) %collective-permute-start.19) | collective-permute-done | bytes 327712 | tf_op jit(solution)/shard_map/ppermute | solution.py:330
  81.6 1.1 %shard_map.77 = bf16[640,512]{1,0:T(8,128)(2,1)} custom-call(f32[512,640]{1,0:T(8,128)S(1)} %shard_map.74.own_ref, bf16[256,640]{1,0:T(8,128)(2,1)S(1)} %collective-permute-done.18.sum_r, bf16[256,640]{1,0:T(8,128)(2,1)S(1)} %collective-permute-done.19.sum_l), custom_call_target="tpu_custom_call" | custom-call | flops 1048576 | bytes 4194304 | tf_op jit(solution)/shard_map/pallas_call | solution.py:436
  (11 shorter events, 0.1 us)
Async XLA Ops:
  0.0 16.3 %copy-start.1 = (bf16[512,128]{1,0:T(8,128)(2,1)S(1)}, bf16[512,128]{1,0:T(8,128)(2,1)}, u32[]{:S(2)}) copy-start(bf16[512,128]{1,0:T(8,128)(2,1)} %key_ref) | copy-start | bytes 393220
  0.0 16.3 %copy-start.2 = (bf16[512,128]{1,0:T(8,128)(2,1)S(1)}, bf16[512,128]{1,0:T(8,128)(2,1)}, u32[]{:S(2)}) copy-start(bf16[512,128]{1,0:T(8,128)(2,1)} %value_ref.1) | copy-start | bytes 393220
  0.0 16.3 %copy-start = (bf16[512,640]{1,0:T(8,128)(2,1)S(1)}, bf16[512,640]{1,0:T(8,128)(2,1)}, u32[]{:S(2)}) copy-start(bf16[512,640]{1,0:T(8,128)(2,1)} %query_ref.11) | copy-start | bytes 1966084
  2.1 10.8 %collective-permute-start.1 = (bf16[528,256]{1,0:T(8,128)(2,1)}, bf16[528,256]{1,0:T(8,128)(2,1)S(1)}, u32[]{:S(2)}, u32[]{:S(2)}) collective-permute-start(bf16[528,256]{1,0:T(8,128)(2,1)} %get-tuple-element.32.own_ref), channel_id=1, source_target_pairs={{0,8},{8,16},{16,24},{24,0},{32,40},{40,48},{48,56},{56,32},{64,72... | collective-permute-start | bytes 811016 | tf_op jit(solution)/shard_map/ppermute | solution.py:330
  4.0 8.8 %collective-permute-start.4 = (bf16[528,256]{1,0:T(8,128)(2,1)}, bf16[528,256]{1,0:T(8,128)(2,1)S(1)}, u32[]{:S(2)}, u32[]{:S(2)}) collective-permute-start(bf16[528,256]{1,0:T(8,128)(2,1)} %get-tuple-element.32.own_ref), channel_id=1, source_target_pairs={{0,24},{8,0},{16,8},{24,16},{32,56},{40,32},{48,40},{56,48},{64,88... | collective-permute-start | bytes 811016 | tf_op jit(solution)/shard_map/ppermute | solution.py:330
  6.2 12.5 %collective-permute-start.3 = (bf16[528,256]{1,0:T(8,128)(2,1)}, bf16[528,256]{1,0:T(8,128)(2,1)S(1)}, u32[]{:S(2)}, u32[]{:S(2)}) collective-permute-start(bf16[528,256]{1,0:T(8,128)(2,1)} %get-tuple-element.32.own_ref), channel_id=1, source_target_pairs={{0,32},{8,40},{16,48},{24,56},{32,64},{40,72},{48,80},{56,88},{64,... | collective-permute-start | bytes 811016 | tf_op jit(solution)/shard_map/ppermute | solution.py:330
  6.5 12.3 %collective-permute-start = (bf16[528,256]{1,0:T(8,128)(2,1)}, bf16[528,256]{1,0:T(8,128)(2,1)S(1)}, u32[]{:S(2)}, u32[]{:S(2)}) collective-permute-start(bf16[528,256]{1,0:T(8,128)(2,1)} %get-tuple-element.32.own_ref), channel_id=1, source_target_pairs={{0,96},{8,104},{16,112},{24,120},{32,0},{40,8},{48,16},{56,24},{64... | collective-permute-start | bytes 811016 | tf_op jit(solution)/shard_map/ppermute | solution.py:330
  12.9 13.5 %collective-permute-start.6 = (bf16[1056,256]{1,0:T(8,128)(2,1)S(1)}, bf16[1056,256]{1,0:T(8,128)(2,1)S(1)}, u32[]{:S(2)}, u32[]{:S(2)}) collective-permute-start(bf16[1056,256]{1,0:T(8,128)(2,1)S(1)} %pad_maximum_fusion), channel_id=1, source_target_pairs={{0,32},{8,40},{16,48},{24,56},{32,64},{40,72},{48,80},{56,88},{64,... | collective-permute-start | bytes 1622024 | tf_op jit(solution)/shard_map/ppermute | solution.py:330
  13.2 19.8 %collective-permute-start.10 = (bf16[1056,256]{1,0:T(8,128)(2,1)S(1)}, bf16[1056,256]{1,0:T(8,128)(2,1)S(1)}, u32[]{:S(2)}, u32[]{:S(2)}) collective-permute-start(bf16[1056,256]{1,0:T(8,128)(2,1)S(1)} %pad_maximum_fusion), channel_id=1, source_target_pairs={{0,96},{8,104},{16,112},{24,120},{32,0},{40,8},{48,16},{56,24},{64... | collective-permute-start | bytes 1622024 | tf_op jit(solution)/shard_map/ppermute | solution.py:330
  15.0 8.3 %collective-permute-start.2 = (bf16[528,256]{1,0:T(8,128)(2,1)S(1)}, bf16[528,256]{1,0:T(8,128)(2,1)S(1)}, u32[]{:S(2)}, u32[]{:S(2)}) collective-permute-start(bf16[528,256]{1,0:T(8,128)(2,1)S(1)} %collective-permute-done.1.back_ref), channel_id=1, source_target_pairs={{0,8},{8,16},{16,24},{24,0},{32,40},{40,48},{48,56},{56,32},{64,72... | collective-permute-start | bytes 811016 | tf_op jit(solution)/shard_map/ppermute | solution.py:330
  16.3 0.7 copy-start.4
  18.7 5.3 %copy-start.3 = (bf16[528,256]{1,0:T(8,128)(2,1)S(1)}, bf16[528,256]{1,0:T(8,128)(2,1)}, u32[]{:S(2)}) copy-start(bf16[528,256]{1,0:T(8,128)(2,1)} %get-tuple-element.32.own_ref) | copy-start | bytes 811012
  23.3 21.4 %collective-permute-start.5 = (bf16[528,256]{1,0:T(8,128)(2,1)S(1)}, bf16[528,256]{1,0:T(8,128)(2,1)S(1)}, u32[]{:S(2)}, u32[]{:S(2)}) collective-permute-start(bf16[528,256]{1,0:T(8,128)(2,1)S(1)} %collective-permute-done.ahead_ref.ahead0), channel_id=1, source_target_pairs={{0,96},{8,104},{16,112},{24,120},{32,0},{40,8},{48,16},{56,24},{64... | collective-permute-start | bytes 811016 | tf_op jit(solution)/shard_map/ppermute | solution.py:330
  26.5 18.3 %collective-permute-start.7 = (bf16[1056,256]{1,0:T(8,128)(2,1)S(1)}, bf16[1056,256]{1,0:T(8,128)(2,1)S(1)}, u32[]{:S(2)}, u32[]{:S(2)}) collective-permute-start(bf16[1056,256]{1,0:T(8,128)(2,1)S(1)} %collective-permute-done.6.back12), channel_id=1, source_target_pairs={{0,32},{8,40},{16,48},{24,56},{32,64},{40,72},{48,80},{56,88},{64,... | collective-permute-start | bytes 1622024 | tf_op jit(solution)/shard_map/ppermute | solution.py:330
  28.0 12.4 %collective-permute-start.9 = (bf16[528,256]{1,0:T(8,128)(2,1)S(1)}, bf16[528,256]{1,0:T(8,128)(2,1)S(1)}, u32[]{:S(2)}, u32[]{:S(2)}) collective-permute-start(bf16[528,256]{1,0:T(8,128)(2,1)S(1)} %slice.6), channel_id=1, source_target_pairs={{0,24},{8,0},{16,8},{24,16},{32,56},{40,32},{48,40},{56,48},{64,88... | collective-permute-start | bytes 811016 | tf_op jit(solution)/shard_map/ppermute | solution.py:330
  33.1 7.7 %collective-permute-start.11 = (bf16[528,256]{1,0:T(8,128)(2,1)S(1)}, bf16[528,256]{1,0:T(8,128)(2,1)S(1)}, u32[]{:S(2)}, u32[]{:S(2)}) collective-permute-start(bf16[528,256]{1,0:T(8,128)(2,1)S(1)} %slice.8), channel_id=1, source_target_pairs={{0,8},{8,16},{16,24},{24,0},{32,40},{40,48},{48,56},{56,32},{64,72... | collective-permute-start | bytes 811016 | tf_op jit(solution)/shard_map/ppermute | solution.py:330
  33.1 11.6 %collective-permute-start.8 = (bf16[528,256]{1,0:T(8,128)(2,1)S(1)}, bf16[528,256]{1,0:T(8,128)(2,1)S(1)}, u32[]{:S(2)}, u32[]{:S(2)}) collective-permute-start(bf16[528,256]{1,0:T(8,128)(2,1)S(1)} %collective-permute-done.2.far_ref), channel_id=1, source_target_pairs={{0,64},{8,72},{16,80},{24,88},{32,96},{40,104},{48,112},{56,120},{... | collective-permute-start | bytes 811016 | tf_op jit(solution)/shard_map/ppermute | solution.py:330
  40.8 4.0 %copy-start.5 = (f32[1,512]{1,0:T(1,128)S(1)}, f32[1,512]{1,0:T(1,128)}, u32[]{:S(2)}) copy-start(f32[1,512]{1,0:T(1,128)} %get-tuple-element.34.cum_ref) | copy-start | bytes 6148
  40.8 11.0 %slice-start = ((s8[6553600]{0:T(1024)(128)(4,1)}), s8[4194304]{0:T(1024)(128)(4,1)S(1)}, s32[]{:S(2)}) async-start(s8[6553600]{0:T(1024)(128)(4,1)} %bitcast.1), calls=%async_computation | async-start | bytes 8388608
  44.8 7.0 %slice-start.1 = ((s8[6553600]{0:T(1024)(128)(4,1)}), s8[2359296]{0:T(1024)(128)(4,1)S(1)}, s32[]{:S(2)}) async-start(s8[6553600]{0:T(1024)(128)(4,1)} %bitcast.1), calls=%async_computation.1 | async-start | bytes 4718592
  52.6 3.0 %collective-permute-start.15 = (bf16[512,640]{1,0:T(8,128)(2,1)S(1)}, bf16[512,640]{1,0:T(8,128)(2,1)S(1)}, u32[]{:S(2)}, u32[]{:S(2)}) collective-permute-start(bf16[512,640]{1,0:T(8,128)(2,1)S(1)} %shard_map.71), channel_id=1, source_target_pairs={{0,1},{1,0},{2,3},{3,2},{4,5},{5,4},{6,7},{7,6},{8,9},{9,8},{10,11... | collective-permute-start | bytes 1966088 | tf_op jit(solution)/shard_map/ppermute | solution.py:330
  55.0 4.1 %collective-permute-start.12 = (bf16[3,512,640]{2,1,0:T(8,128)(2,1)S(1)}, bf16[3,512,640]{2,1,0:T(8,128)(2,1)S(1)}, u32[]{:S(2)}, u32[]{:S(2)}) collective-permute-start(bf16[3,512,640]{2,1,0:T(8,128)(2,1)S(1)} %shard_map.72), channel_id=1, source_target_pairs={{0,1},{1,0},{2,3},{3,2},{4,5},{5,4},{6,7},{7,6},{8,9},{9,8},{10,11... | collective-permute-start | bytes 5898248 | tf_op jit(solution)/shard_map/ppermute | solution.py:330
  56.3 10.6 %collective-permute-start.16 = (bf16[256,640]{1,0:T(8,128)(2,1)S(1)}, bf16[256,640]{1,0:T(8,128)(2,1)S(1)}, u32[]{:S(2)}, u32[]{:S(2)}) collective-permute-start(bf16[256,640]{1,0:T(8,128)(2,1)S(1)} %get-tuple-element.54), channel_id=1, source_target_pairs={{0,2},{1,3},{2,4},{3,5},{4,6},{5,7},{6,0},{7,1},{8,10},{9,11},{10,... | collective-permute-start | bytes 983048 | tf_op jit(solution)/shard_map/ppermute | solution.py:330
  56.9 11.8 %collective-permute-start.17 = (bf16[256,640]{1,0:T(8,128)(2,1)S(1)}, bf16[256,640]{1,0:T(8,128)(2,1)S(1)}, u32[]{:S(2)}, u32[]{:S(2)}) collective-permute-start(bf16[256,640]{1,0:T(8,128)(2,1)S(1)} %get-tuple-element.56), channel_id=1, source_target_pairs={{0,6},{1,7},{2,0},{3,1},{4,2},{5,3},{6,4},{7,5},{8,14},{9,15},{10,... | collective-permute-start | bytes 983048 | tf_op jit(solution)/shard_map/ppermute | solution.py:330
  61.1 12.9 %collective-permute-start.13 = (bf16[256,640]{1,0:T(8,128)(2,1)S(1)}, bf16[256,640]{1,0:T(8,128)(2,1)S(1)}, u32[]{:S(2)}, u32[]{:S(2)}) collective-permute-start(bf16[256,640]{1,0:T(8,128)(2,1)S(1)} %get-tuple-element.50), channel_id=1, source_target_pairs={{0,2},{1,3},{2,4},{3,5},{4,6},{5,7},{6,0},{7,1},{8,10},{9,11},{10,... | collective-permute-start | bytes 983048 | tf_op jit(solution)/shard_map/ppermute | solution.py:330
  62.2 13.6 %collective-permute-start.14 = (bf16[256,640]{1,0:T(8,128)(2,1)S(1)}, bf16[256,640]{1,0:T(8,128)(2,1)S(1)}, u32[]{:S(2)}, u32[]{:S(2)}) collective-permute-start(bf16[256,640]{1,0:T(8,128)(2,1)S(1)} %get-tuple-element.51), channel_id=1, source_target_pairs={{0,6},{1,7},{2,0},{3,1},{4,2},{5,3},{6,4},{7,5},{8,14},{9,15},{10,... | collective-permute-start | bytes 983048 | tf_op jit(solution)/shard_map/ppermute | solution.py:330
  68.8 11.3 %collective-permute-start.18 = (bf16[256,640]{1,0:T(8,128)(2,1)S(1)}, bf16[256,640]{1,0:T(8,128)(2,1)S(1)}, u32[]{:S(2)}, u32[]{:S(2)}) collective-permute-start(bf16[256,640]{1,0:T(8,128)(2,1)S(1)} %get-tuple-element.57), channel_id=1, source_target_pairs={{0,2},{1,3},{2,4},{3,5},{4,6},{5,7},{6,0},{7,1},{8,10},{9,11},{10,... | collective-permute-start | bytes 983048 | tf_op jit(solution)/shard_map/ppermute | solution.py:330
  69.2 12.4 %collective-permute-start.19 = (bf16[256,640]{1,0:T(8,128)(2,1)S(1)}, bf16[256,640]{1,0:T(8,128)(2,1)S(1)}, u32[]{:S(2)}, u32[]{:S(2)}) collective-permute-start(bf16[256,640]{1,0:T(8,128)(2,1)S(1)} %get-tuple-element.58), channel_id=1, source_target_pairs={{0,6},{1,7},{2,0},{3,1},{4,2},{5,3},{6,4},{7,5},{8,14},{9,15},{10,... | collective-permute-start | bytes 983048 | tf_op jit(solution)/shard_map/ppermute | solution.py:330

commit v2 on v1

--- a/solution.py
+++ b/solution.py
@@ -11,6 +11,7 @@
 PAY = TOK + 16
 SIDE = 4
 CHUNK = 640
+SPLIT = TOK // 2
 BF = jnp.bfloat16
 F32 = jnp.float32
 VMEM = pl.BlockSpec(memory_space=pltpu.VMEM)
@@ -237,8 +238,8 @@
 
 
 def last_body(
-    query_ref, far0, far12, far3, stat_ref, acc_in, own_ref, cum_ref, gain_ref,
-    out_ref, acc, keys, values
+    query_ref, far0, far12, far3, stat_ref, acc_in, own_ref, cum_ref, gain_ref, weight_ref,
+    out_ref, other_ref, acc, keys, values
 ):
     index = lax.axis_index("ctx")
     place_y, places = index // SIDE, slot_places(index % SIDE)
@@ -256,9 +257,7 @@
 
     @pl.when(place_y >= 2)
     def _():
-        @pl.loop(0, 2)
-        def _(i):
-            attend(query_ref, keys, values, i * 2 * TOK, 2 * TOK, acc)
+        attend(query_ref, keys, values, 0, SIDE * TOK, acc)
 
     grow = jnp.exp(column(cum_ref[...]))
     for head in range(GROUP_HEADS):
@@ -266,6 +265,7 @@
         number = own_ref[:, cols] + grow * acc[:, cols]
         mean = jnp.mean(number * number, axis=-1, keepdims=True)
         out_ref[:, cols] = (number * lax.rsqrt(mean + 1e-06) * gain_ref[0:1, cols]).astype(BF)
+    other_ref[...] = product(out_ref, weight_ref, 2, 1).astype(BF)
 
 
 def features_of(weight_ref, step, flip):
@@ -278,10 +278,6 @@
     return jnp.dot(
         normed_ref[...], features_of(weight_ref, step, flip), preferred_element_type=F32
     )
-
-
-def other_far_body(normed_ref, weight_ref, out_ref):
-    out_ref[...] = product(normed_ref, weight_ref, 2, 1).astype(BF)
 
 
 def other_near_body(normed_ref, weight_ref, out_ref):
@@ -292,20 +288,18 @@
 
 
 def mine_far_body(normed_ref, weight_ref, other_ref, far_r, far_l):
-    half = TOK // 2
     both = product(normed_ref, weight_ref, 2, 0) + other_ref[...].astype(F32)
-    far_r[...] = both[:half].astype(BF)
-    far_l[...] = both[half:].astype(BF)
+    far_r[...] = both[:SPLIT].astype(BF)
+    far_l[...] = both[SPLIT:].astype(BF)
 
 
 def mine_near_body(normed_ref, weight_ref, other_ref, near_r, near_l, hold_r, hold_l, own_ref):
-    half = TOK // 2
     both = product(normed_ref, weight_ref, 1, 0) + other_ref[0].astype(F32)
-    hold_r[...] = both[:half]
-    near_r[...] = both[half:].astype(BF)
+    hold_r[...] = both[:SPLIT]
+    near_r[...] = both[SPLIT:].astype(BF)
     both = product(normed_ref, weight_ref, 3, 0) + other_ref[1].astype(F32)
-    near_l[...] = both[:half].astype(BF)
-    hold_l[...] = both[half:]
+    near_l[...] = both[:SPLIT].astype(BF)
+    hold_l[...] = both[SPLIT:]
     own_ref[...] = product(normed_ref, weight_ref, 0, 0) + other_ref[2].astype(F32)
 
 
@@ -315,15 +309,13 @@
 
 
 def gather_body(own_ref, near_r, near_l, out_ref):
-    half = TOK // 2
-    out_ref[:half, :] = own_ref[:half, :] + near_l[...].astype(F32)
-    out_ref[half:, :] = own_ref[half:, :] + near_r[...].astype(F32)
+    near = jnp.concatenate([near_l[...], near_r[...]], axis=0).astype(F32)
+    out_ref[...] = (own_ref[...] + near).T
 
 
 def finish_body(own_ref, sum_r, sum_l, out_ref):
-    half = TOK // 2
-    out_ref[:, :half] = (own_ref[:half, :] + sum_r[...].astype(F32)).T.astype(BF)
-    out_ref[:, half:] = (own_ref[half:, :] + sum_l[...].astype(F32)).T.astype(BF)
+    sums = jnp.concatenate([sum_r[...], sum_l[...]], axis=0)
+    out_ref[...] = (own_ref[...] + sums.T.astype(F32)).astype(BF)
 
 
 def send(value, axis, pairs):
@@ -390,21 +382,18 @@
         scratch(2),
         in_specs=[VMEM] * 10,
     )(queries, back0, back12, back3, ahead0, ahead12, ahead3, stat, acc, groups)
-    normed = kernel_call(
+    chunk_flops = 2 * TOK * CHUNK * wide
+    chunk = shape((TOK, CHUNK), BF)
+    long_bf, long_f32 = shape((SPLIT, CHUNK), BF), shape((SPLIT, CHUNK), F32)
+    short_bf, short_f32 = shape((TOK - SPLIT, CHUNK), BF), shape((TOK - SPLIT, CHUNK), F32)
+    normed, other_far = kernel_call(
         last_body,
-        shape((TOK, wide), BF),
+        (shape((TOK, wide), BF), chunk),
         4 * block_flops,
         2**22,
         [pltpu.VMEM((TOK, wide), F32), *scratch(4)],
-        in_specs=[VMEM] * 9,
-    )(queries, far0, far12, far3, stat, acc, own, cum, norm_gain.reshape(1, wide))
-
-    chunk_flops = 2 * TOK * CHUNK * wide
-    chunk = shape((TOK, CHUNK), BF)
-    half_bf, half_f32 = shape((TOK // 2, CHUNK), BF), shape((TOK // 2, CHUNK), F32)
-    other_far = kernel_call(other_far_body, chunk, chunk_flops, 2**20, in_specs=[VMEM] * 2)(
-        normed, out_weight
-    )
+        in_specs=[VMEM] * 10,
+    )(queries, far0, far12, far3, stat, acc, own, cum, norm_gain.reshape(1, wide), out_weight)
     normed, other_far = after((normed, other_far))
     other_far = send(other_far, "head", CORE)
     other_near = kernel_call(
@@ -412,26 +401,26 @@
     )(normed, out_weight)
     other_near = send(other_near, "head", CORE)
     far_r, far_l = kernel_call(
-        mine_far_body, (half_bf, half_bf), 30 * chunk_flops, 2**20, in_specs=[VMEM] * 3
+        mine_far_body, (long_bf, short_bf), 30 * chunk_flops, 2**20, in_specs=[VMEM] * 3
     )(normed, out_weight, other_far)
     far_r = send(far_r, "head", HEAD_X[1])
     far_l = send(far_l, "head", HEAD_X[-1])
     near_r, near_l, hold_r, hold_l, own_sum = kernel_call(
         mine_near_body,
-        (half_bf, half_bf, half_f32, half_f32, shape((TOK, CHUNK), F32)),
+        (short_bf, long_bf, long_f32, short_f32, shape((TOK, CHUNK), F32)),
         3 * chunk_flops,
         2**22,
         in_specs=[VMEM] * 3,
     )(normed, out_weight, other_near)
     near_r = send(near_r, "head", HEAD_X[1])
     near_l = send(near_l, "head", HEAD_X[-1])
-    sum_r, sum_l = kernel_call(pass_body, (half_bf,) * 2, 2**19, 2**21, in_specs=[VMEM] * 4)(
+    sum_r, sum_l = kernel_call(pass_body, (long_bf, short_bf), 2**19, 2**21, in_specs=[VMEM] * 4)(
         hold_r, far_r, hold_l, far_l
     )
     sum_r = send(sum_r, "head", HEAD_X[1])
     sum_l = send(sum_l, "head", HEAD_X[-1])
     own_sum = kernel_call(
-        gather_body, shape((TOK, CHUNK), F32), 2**20, 2**22, in_specs=[VMEM] * 3
+        gather_body, shape((CHUNK, TOK), F32), 2**20, 2**22, in_specs=[VMEM] * 3
     )(own_sum, near_r, near_l)
     return kernel_call(finish_body, shape((CHUNK, TOK), BF), 2**20, 2**22, in_specs=[VMEM] * 3)(
         own_sum, sum_r, sum_l

time: 82.9 us -> 82.9 us (level)
    pallas_call x6 -> x5, Pallas kernels: 10.7 us -> 10.8 us  [the longest x1 7.58 us: per_device(): kernel_call(last_body, (shape((TOK, wide), BF), chunk), 4 * block_flops,...]
  transfers between devices with their start and end apart: 20 -> 20, of which waited for: 11 -> 11; matrix products, arithmetic and copies ran while one was open for 1% -> 1% of each run, Pallas kernels for 26% -> 27%
where the time goes in v2:
time: 82.9 us; the launch traced here: 82.7 us
  Pallas kernels  32.7 us (39%)
  starting transfers between devices  24.4 us (29%)
  waiting for transfers between devices  23.9 us (29%)
  local copies, waits for them, and re-layouts  1.43 us (2%)
    ppermute x20, starting transfers between devices, send(): return lax.ppermute(value, axis, pairs)  24.4 us
    ppermute x20, waiting for transfers between devices, send(): return lax.ppermute(value, axis, pairs)  23.9 us
    pallas_call x1, Pallas kernels, per_device(): kernel_call(last_body, (shape((TOK, wide), BF), chunk), 4 * block_flops,...  7.58 us
    pallas_call x1, Pallas kernels, per_device(): kernel_call(middle_body, shape((2, 2, TOK, wide), F32), 24 * block_flops,...  6.98 us
    pallas_call x1, Pallas kernels, per_device(): kernel_call(near_body, (shape((2, TOK, wide), F32), stat_shape), 2 * bloc...  4 us
    pallas_call x1, Pallas kernels, per_device(): kernel_call(first_body, shape((2, TOK, wide), F32), 2 * block_flops, 2 **...  3.36 us
    pallas_call x1, Pallas kernels, per_device(): kernel_call(other_near_body, shape((3, TOK, CHUNK), BF), 30 * chunk_flops...  2.33 us
    pallas_call x1, Pallas kernels, per_device(): kernel_call(prepare_body, (shape((PAY, 2 * HEAD_DIM), BF), shape((1, TOK)...  2.04 us
  transfers between devices with their start and end apart: 20, of which 11 were waited for; matrix products, arithmetic and copies ran while one was open for 1% of the time, Pallas kernels for 27%

profile of v2, /device:TPU:30, one launch (start us, length us, event | category | flops | bytes accessed | tf_op | source)
XLA Modules:
  0.0 82.7 jit_solution(11920865330918554031)
XLA Ops:
  0.0 2.0 %shard_map.64 = (bf16[528,256]{1,0:T(8,128)(2,1)}, f32[1,512]{1,0:T(1,128)}) custom-call(bf16[512,128]{1,0:T(8,128)(2,1)} %key_ref, bf16[512,128]{1,0:T(8,128)(2,1)} %value_ref.1, f32[1,512]{1,0:T(1,128)} %bitcast.3), custom_call_target="tpu_custom_call" | custom-call | flops 8388608 | bytes 524288 | tf_op jit(solution)/shard_map/pallas_call | solution.py:328
  2.1 2.0 %collective-permute-start.1 = (bf16[528,256]{1,0:T(8,128)(2,1)}, bf16[528,256]{1,0:T(8,128)(2,1)S(1)}, u32[]{:S(2)}, u32[]{:S(2)}) collective-permute-start(bf16[528,256]{1,0:T(8,128)(2,1)} %get-tuple-element.32.own_ref), channel_id=1, source_target_pairs={{0,8},{8,16},{16,24},{24,0},{32,40},{40,48},{48,56},{56,32},{64,72... | collective-permute-start | bytes 811016 | tf_op jit(solution)/shard_map/ppermute | solution.py:322
  4.0 2.2 %collective-permute-start.4 = (bf16[528,256]{1,0:T(8,128)(2,1)}, bf16[528,256]{1,0:T(8,128)(2,1)S(1)}, u32[]{:S(2)}, u32[]{:S(2)}) collective-permute-start(bf16[528,256]{1,0:T(8,128)(2,1)} %get-tuple-element.32.own_ref), channel_id=1, source_target_pairs={{0,24},{8,0},{16,8},{24,16},{32,56},{40,32},{48,40},{56,48},{64,88... | collective-permute-start | bytes 811016 | tf_op jit(solution)/shard_map/ppermute | solution.py:322
  6.2 0.2 collective-permute-start.3
  6.5 1.8 %collective-permute-start = (bf16[528,256]{1,0:T(8,128)(2,1)}, bf16[528,256]{1,0:T(8,128)(2,1)S(1)}, u32[]{:S(2)}, u32[]{:S(2)}) collective-permute-start(bf16[528,256]{1,0:T(8,128)(2,1)} %get-tuple-element.32.own_ref), channel_id=1, source_target_pairs={{0,96},{8,104},{16,112},{24,120},{32,0},{40,8},{48,16},{56,24},{64... | collective-permute-start | bytes 811016 | tf_op jit(solution)/shard_map/ppermute | solution.py:322
  8.3 0.7 reshape.7.gain_ref
  9.0 3.9 %collective-permute-done.1.back_ref = bf16[528,256]{1,0:T(8,128)(2,1)S(1)} collective-permute-done((bf16[528,256]{1,0:T(8,128)(2,1)}, bf16[528,256]{1,0:T(8,128)(2,1)S(1)}, u32[]{:S(2)}, u32[]{:S(2)}) %collective-permute-start.1) | collective-permute-done | bytes 270368 | tf_op jit(solution)/shard_map/ppermute | solution.py:322
  12.9 0.0 collective-permute-done.4.ahead_ref
  12.9 0.3 collective-permute-start.6
  13.2 1.8 %collective-permute-start.10 = (bf16[1056,256]{1,0:T(8,128)(2,1)S(1)}, bf16[1056,256]{1,0:T(8,128)(2,1)S(1)}, u32[]{:S(2)}, u32[]{:S(2)}) collective-permute-start(bf16[1056,256]{1,0:T(8,128)(2,1)S(1)} %pad_maximum_fusion), channel_id=1, source_target_pairs={{0,96},{8,104},{16,112},{24,120},{32,0},{40,8},{48,16},{56,24},{64... | collective-permute-start | bytes 1622024 | tf_op jit(solution)/shard_map/ppermute | solution.py:322
  15.0 1.3 %collective-permute-start.2 = (bf16[528,256]{1,0:T(8,128)(2,1)S(1)}, bf16[528,256]{1,0:T(8,128)(2,1)S(1)}, u32[]{:S(2)}, u32[]{:S(2)}) collective-permute-start(bf16[528,256]{1,0:T(8,128)(2,1)S(1)} %collective-permute-done.1.back_ref), channel_id=1, source_target_pairs={{0,8},{8,16},{16,24},{24,0},{32,40},{40,48},{48,56},{56,32},{64,72... | collective-permute-start | bytes 811016 | tf_op jit(solution)/shard_map/ppermute | solution.py:322
  16.2 0.0 copy-done.1
  16.3 0.0 copy-done.2
  16.3 0.0 copy-done
  16.3 0.7 copy-done.3
  16.9 1.8 %shard_map.65.own_ref = f32[512,640]{1,0:T(8,128)S(1)} custom-call(bf16[512,640]{1,0:T(8,128)(2,1)S(1)} %copy-done, bf16[512,128]{1,0:T(8,128)(2,1)S(1)} %copy-done.1, bf16[512,128]{1,0:T(8,128)(2,1)S(1)} %copy-done.2, f32[1,512]{1,0:T(1,128)S(1)} %copy-done.3), custom_call_target="tpu_custom_call" | custom-call | flops 5368709120 | bytes 2097152 | tf_op jit(solution)/shard_map/pallas_call | solution.py:350
  18.7 0.0 copy-start.5
  18.7 0.0 collective-permute-done.3.back_ref.back0
  18.7 0.0 collective-permute-done.ahead_ref.ahead0
  18.8 3.4 %shard_map.66.first_ref = f32[2,512,640]{2,1,0:T(8,128)S(1)} custom-call(bf16[512,640]{1,0:T(8,128)(2,1)S(1)} %copy-done, bf16[528,256]{1,0:T(8,128)(2,1)S(1)} %collective-permute-done.3.back_ref.back0, bf16[528,256]{1,0:T(8,128)(2,1)S(1)} %collective-permute-done.ahead_ref.ahead0), custom_call_target="tpu_custom_call" | custom-call | flops 1342177280 | bytes 2097152 | tf_op jit(solution)/shard_map/pallas_call | solution.py:356
  22.1 1.2 %collective-permute-done.2.far_ref = bf16[528,256]{1,0:T(8,128)(2,1)S(1)} collective-permute-done((bf16[528,256]{1,0:T(8,128)(2,1)S(1)}, bf16[528,256]{1,0:T(8,128)(2,1)S(1)}, u32[]{:S(2)}, u32[]{:S(2)}) %collective-permute-start.2) | collective-permute-done | bytes 270368 | tf_op jit(solution)/shard_map/ppermute | solution.py:322
  23.3 0.7 collective-permute-start.5
  24.1 0.0 copy-done.5
  24.1 0.3 shard_map.67
  24.4 2.1 %collective-permute-done.6.back12 = bf16[1056,256]{1,0:T(8,128)(2,1)S(1)} collective-permute-done((bf16[1056,256]{1,0:T(8,128)(2,1)S(1)}, bf16[1056,256]{1,0:T(8,128)(2,1)S(1)}, u32[]{:S(2)}, u32[]{:S(2)}) %collective-permute-start.6) | collective-permute-done | bytes 540704 | tf_op jit(solution)/shard_map/ppermute | solution.py:322
  26.5 1.6 %collective-permute-start.7 = (bf16[1056,256]{1,0:T(8,128)(2,1)S(1)}, bf16[1056,256]{1,0:T(8,128)(2,1)S(1)}, u32[]{:S(2)}, u32[]{:S(2)}) collective-permute-start(bf16[1056,256]{1,0:T(8,128)(2,1)S(1)} %collective-permute-done.6.back12), channel_id=1, source_target_pairs={{0,32},{8,40},{16,48},{24,56},{32,64},{40,72},{48,80},{56,88},{64,... | collective-permute-start | bytes 1622024 | tf_op jit(solution)/shard_map/ppermute | solution.py:322
  28.0 5.0 %collective-permute-start.9 = (bf16[528,256]{1,0:T(8,128)(2,1)S(1)}, bf16[528,256]{1,0:T(8,128)(2,1)S(1)}, u32[]{:S(2)}, u32[]{:S(2)}) collective-permute-start(bf16[528,256]{1,0:T(8,128)(2,1)S(1)} %slice.6), channel_id=1, source_target_pairs={{0,24},{8,0},{16,8},{24,16},{32,56},{40,32},{48,40},{56,48},{64,88... | collective-permute-start | bytes 811016 | tf_op jit(solution)/shard_map/ppermute | solution.py:322
  33.1 0.0 collective-permute-done.10.ahead12
  33.1 0.0 slice-start.1
  33.1 0.1 collective-permute-start.11
  33.2 0.3 collective-permute-start.8
  33.5 7.0 %shard_map.68.groups = f32[2,2,512,640]{3,2,1,0:T(8,128)S(1)} custom-call(bf16[512,640]{1,0:T(8,128)(2,1)S(1)} %copy-done, bf16[528,256]{1,0:T(8,128)(2,1)S(1)} %collective-permute-done.3.back_ref.back0, bf16[1056,256]{1,0:T(8,128)(2,1)S(1)} %collective-permute-done.6.back12, bf16[528,256]{1,0:T(8,128)(2,1)S(1)} %collective-permute-done.ahead_ref.ahead0, ...), custom_call_target="tpu_custom_call" | custom-call | flops 16106127360 | bytes 4194304 | tf_op jit(solution)/shard_map/pallas_call | solution.py:369
  40.4 0.0 collective-permute-done.9.back3
  40.5 0.4 collective-permute-done.11.ahead3
  40.8 4.0 %shard_map.69 = (f32[2,512,640]{2,1,0:T(8,128)S(1)}, f32[8,128]{1,0:T(8,128)S(1)}) custom-call(bf16[512,640]{1,0:T(8,128)(2,1)S(1)} %copy-done, bf16[528,256]{1,0:T(8,128)(2,1)S(1)} %collective-permute-done.3.back_ref.back0, bf16[1056,256]{1,0:T(8,128)(2,1)S(1)} %collective-permute-done.6.back12, bf16[528,256]{1,0:T(8,128)(2,1)S(1)} %collective-permute-done.9.back3, ...), custom_call_target="tpu_custom_call" | custom-call | flops 1342177280 | bytes 4194304 | tf_op jit(solution)/shard_map/pallas_call | solution.py:377
  44.8 0.0 collective-permute-done.5.far0
  44.9 0.0 collective-permute-done.8.far3
  44.9 0.0 collective-permute-done.7.far12
  44.9 0.0 slice-done
  44.9 0.0 slice-done.1
  44.9 0.0 copy-done.4
  44.9 7.6 %shard_map.70 = (bf16[512,640]{1,0:T(8,128)(2,1)S(1)}, bf16[512,640]{1,0:T(8,128)(2,1)S(1)}) custom-call(bf16[512,640]{1,0:T(8,128)(2,1)S(1)} %copy-done, bf16[528,256]{1,0:T(8,128)(2,1)S(1)} %collective-permute-done.5.far0, bf16[1056,256]{1,0:T(8,128)(2,1)S(1)} %collective-permute-done.7.far12, bf16[528,256]{1,0:T(8,128)(2,1)S(1)} %collective-permute-done.8.far3, ...), custom_call_target="tpu_custom_call" | custom-call | flops 2684354560 | bytes 4194304 | tf_op jit(solution)/shard_map/pallas_call | solution.py:389
  52.5 0.3 collective-permute-start.15
  52.8 2.3 %shard_map.71 = bf16[3,512,640]{2,1,0:T(8,128)(2,1)S(1)} custom-call(bf16[512,640]{1,0:T(8,128)(2,1)S(1)} %get-tuple-element.48.normed_ref, bf16[640,5120]{1,0:T(8,128)(2,1)S(1)} %bitcast.2), custom_call_target="tpu_custom_call" | custom-call | flops 12582912000 | bytes 2097152 | tf_op jit(solution)/shard_map/pallas_call | solution.py:399
  55.2 0.6 collective-permute-start.12
  55.7 0.0 collective-permute-done.15.other_ref
  55.7 0.8 shard_map.74
  56.5 0.5 collective-permute-start.16
  57.0 1.6 %collective-permute-start.17 = (bf16[256,640]{1,0:T(8,128)(2,1)S(1)}, bf16[256,640]{1,0:T(8,128)(2,1)S(1)}, u32[]{:S(2)}, u32[]{:S(2)}) collective-permute-start(bf16[256,640]{1,0:T(8,128)(2,1)S(1)} %get-tuple-element.56), channel_id=1, source_target_pairs={{0,6},{1,7},{2,0},{3,1},{4,2},{5,3},{6,4},{7,5},{8,14},{9,15},{10,... | collective-permute-start | bytes 983048 | tf_op jit(solution)/shard_map/ppermute | solution.py:322
  58.6 0.7 collective-permute-done.12.other_ref
  59.3 2.0 %shard_map.72 = (bf16[256,640]{1,0:T(8,128)(2,1)S(1)}, bf16[256,640]{1,0:T(8,128)(2,1)S(1)}, f32[256,640]{1,0:T(8,128)S(1)}, f32[256,640]{1,0:T(8,128)S(1)}, f32[512,640]{1,0:T(8,128)S(1)}) custom-call(bf16[512,640]{1,0:T(8,128)(2,1)S(1)} %get-tuple-element.48.normed_ref, bf16[640,5120]{1,0:T(8,128)(2,1)S(1)} %bitcast.2, ...), custom_call_target="tpu_custom_call" | custom-call | flops 1258291200 | bytes 4194304 | tf_op jit(solution)/shard_map/pallas_call | solution.py:408
  61.3 1.0 %collective-permute-start.13 = (bf16[256,640]{1,0:T(8,128)(2,1)S(1)}, bf16[256,640]{1,0:T(8,128)(2,1)S(1)}, u32[]{:S(2)}, u32[]{:S(2)}) collective-permute-start(bf16[256,640]{1,0:T(8,128)(2,1)S(1)} %get-tuple-element.50), channel_id=1, source_target_pairs={{0,2},{1,3},{2,4},{3,5},{4,6},{5,7},{6,0},{7,1},{8,10},{9,11},{10,... | collective-permute-start | bytes 983048 | tf_op jit(solution)/shard_map/ppermute | solution.py:322
  62.3 1.1 %collective-permute-start.14 = (bf16[256,640]{1,0:T(8,128)(2,1)S(1)}, bf16[256,640]{1,0:T(8,128)(2,1)S(1)}, u32[]{:S(2)}, u32[]{:S(2)}) collective-permute-start(bf16[256,640]{1,0:T(8,128)(2,1)S(1)} %get-tuple-element.51), channel_id=1, source_target_pairs={{0,6},{1,7},{2,0},{3,1},{4,2},{5,3},{6,4},{7,5},{8,14},{9,15},{10,... | collective-permute-start | bytes 983048 | tf_op jit(solution)/shard_map/ppermute | solution.py:322
  63.4 3.7 %collective-permute-done.16.far_r = bf16[256,640]{1,0:T(8,128)(2,1)S(1)} collective-permute-done((bf16[256,640]{1,0:T(8,128)(2,1)S(1)}, bf16[256,640]{1,0:T(8,128)(2,1)S(1)}, u32[]{:S(2)}, u32[]{:S(2)}) %collective-permute-start.16) | collective-permute-done | bytes 327712 | tf_op jit(solution)/shard_map/ppermute | solution.py:322
  67.1 1.7 %collective-permute-done.17.far_l = bf16[256,640]{1,0:T(8,128)(2,1)S(1)} collective-permute-done((bf16[256,640]{1,0:T(8,128)(2,1)S(1)}, bf16[256,640]{1,0:T(8,128)(2,1)S(1)}, u32[]{:S(2)}, u32[]{:S(2)}) %collective-permute-start.17) | collective-permute-done | bytes 327712 | tf_op jit(solution)/shard_map/ppermute | solution.py:322
  68.9 0.1 shard_map.75
  69.0 0.4 collective-permute-start.18
  69.3 1.7 %collective-permute-start.19 = (bf16[256,640]{1,0:T(8,128)(2,1)S(1)}, bf16[256,640]{1,0:T(8,128)(2,1)S(1)}, u32[]{:S(2)}, u32[]{:S(2)}) collective-permute-start(bf16[256,640]{1,0:T(8,128)(2,1)S(1)} %get-tuple-element.58), channel_id=1, source_target_pairs={{0,6},{1,7},{2,0},{3,1},{4,2},{5,3},{6,4},{7,5},{8,14},{9,15},{10,... | collective-permute-start | bytes 983048 | tf_op jit(solution)/shard_map/ppermute | solution.py:322
  71.1 3.1 %collective-permute-done.13.near_r = bf16[256,640]{1,0:T(8,128)(2,1)S(1)} collective-permute-done((bf16[256,640]{1,0:T(8,128)(2,1)S(1)}, bf16[256,640]{1,0:T(8,128)(2,1)S(1)}, u32[]{:S(2)}, u32[]{:S(2)}) %collective-permute-start.13) | collective-permute-done | bytes 327712 | tf_op jit(solution)/shard_map/ppermute | solution.py:322
  74.2 1.7 %collective-permute-done.14.near_l = bf16[256,640]{1,0:T(8,128)(2,1)S(1)} collective-permute-done((bf16[256,640]{1,0:T(8,128)(2,1)S(1)}, bf16[256,640]{1,0:T(8,128)(2,1)S(1)}, u32[]{:S(2)}, u32[]{:S(2)}) %collective-permute-start.14) | collective-permute-done | bytes 327712 | tf_op jit(solution)/shard_map/ppermute | solution.py:322
  75.9 0.4 shard_map.73.own_ref
  76.3 4.0 %collective-permute-done.18.sum_r = bf16[256,640]{1,0:T(8,128)(2,1)S(1)} collective-permute-done((bf16[256,640]{1,0:T(8,128)(2,1)S(1)}, bf16[256,640]{1,0:T(8,128)(2,1)S(1)}, u32[]{:S(2)}, u32[]{:S(2)}) %collective-permute-start.18) | collective-permute-done | bytes 327712 | tf_op jit(solution)/shard_map/ppermute | solution.py:322
  80.3 1.4 %collective-permute-done.19.sum_l = bf16[256,640]{1,0:T(8,128)(2,1)S(1)} collective-permute-done((bf16[256,640]{1,0:T(8,128)(2,1)S(1)}, bf16[256,640]{1,0:T(8,128)(2,1)S(1)}, u32[]{:S(2)}, u32[]{:S(2)}) %collective-permute-start.19) | collective-permute-done | bytes 327712 | tf_op jit(solution)/shard_map/ppermute | solution.py:322
  81.7 1.1 %shard_map.76 = bf16[640,512]{1,0:T(8,128)(2,1)} custom-call(f32[640,512]{1,0:T(8,128)S(1)} %shard_map.73.own_ref, bf16[256,640]{1,0:T(8,128)(2,1)S(1)} %collective-permute-done.18.sum_r, bf16[256,640]{1,0:T(8,128)(2,1)S(1)} %collective-permute-done.19.sum_l), custom_call_target="tpu_custom_call" | custom-call | flops 1048576 | bytes 4194304 | tf_op jit(solution)/shard_map/pallas_call | solution.py:425
  (10 shorter events, 0.1 us)
Async XLA Ops:
  0.0 16.3 %copy-start.1 = (bf16[512,128]{1,0:T(8,128)(2,1)S(1)}, bf16[512,128]{1,0:T(8,128)(2,1)}, u32[]{:S(2)}) copy-start(bf16[512,128]{1,0:T(8,128)(2,1)} %key_ref) | copy-start | bytes 393220
  0.0 16.3 %copy-start.2 = (bf16[512,128]{1,0:T(8,128)(2,1)S(1)}, bf16[512,128]{1,0:T(8,128)(2,1)}, u32[]{:S(2)}) copy-start(bf16[512,128]{1,0:T(8,128)(2,1)} %value_ref.1) | copy-start | bytes 393220
  0.0 16.3 %copy-start = (bf16[512,640]{1,0:T(8,128)(2,1)S(1)}, bf16[512,640]{1,0:T(8,128)(2,1)}, u32[]{:S(2)}) copy-start(bf16[512,640]{1,0:T(8,128)(2,1)} %query_ref.11) | copy-start | bytes 1966084
  2.1 10.8 %collective-permute-start.1 = (bf16[528,256]{1,0:T(8,128)(2,1)}, bf16[528,256]{1,0:T(8,128)(2,1)S(1)}, u32[]{:S(2)}, u32[]{:S(2)}) collective-permute-start(bf16[528,256]{1,0:T(8,128)(2,1)} %get-tuple-element.32.own_ref), channel_id=1, source_target_pairs={{0,8},{8,16},{16,24},{24,0},{32,40},{40,48},{48,56},{56,32},{64,72... | collective-permute-start | bytes 811016 | tf_op jit(solution)/shard_map/ppermute | solution.py:322
  4.0 8.8 %collective-permute-start.4 = (bf16[528,256]{1,0:T(8,128)(2,1)}, bf16[528,256]{1,0:T(8,128)(2,1)S(1)}, u32[]{:S(2)}, u32[]{:S(2)}) collective-permute-start(bf16[528,256]{1,0:T(8,128)(2,1)} %get-tuple-element.32.own_ref), channel_id=1, source_target_pairs={{0,24},{8,0},{16,8},{24,16},{32,56},{40,32},{48,40},{56,48},{64,88... | collective-permute-start | bytes 811016 | tf_op jit(solution)/shard_map/ppermute | solution.py:322
  6.2 12.5 %collective-permute-start.3 = (bf16[528,256]{1,0:T(8,128)(2,1)}, bf16[528,256]{1,0:T(8,128)(2,1)S(1)}, u32[]{:S(2)}, u32[]{:S(2)}) collective-permute-start(bf16[528,256]{1,0:T(8,128)(2,1)} %get-tuple-element.32.own_ref), channel_id=1, source_target_pairs={{0,32},{8,40},{16,48},{24,56},{32,64},{40,72},{48,80},{56,88},{64,... | collective-permute-start | bytes 811016 | tf_op jit(solution)/shard_map/ppermute | solution.py:322
  6.5 12.3 %collective-permute-start = (bf16[528,256]{1,0:T(8,128)(2,1)}, bf16[528,256]{1,0:T(8,128)(2,1)S(1)}, u32[]{:S(2)}, u32[]{:S(2)}) collective-permute-start(bf16[528,256]{1,0:T(8,128)(2,1)} %get-tuple-element.32.own_ref), channel_id=1, source_target_pairs={{0,96},{8,104},{16,112},{24,120},{32,0},{40,8},{48,16},{56,24},{64... | collective-permute-start | bytes 811016 | tf_op jit(solution)/shard_map/ppermute | solution.py:322
  12.9 13.5 %collective-permute-start.6 = (bf16[1056,256]{1,0:T(8,128)(2,1)S(1)}, bf16[1056,256]{1,0:T(8,128)(2,1)S(1)}, u32[]{:S(2)}, u32[]{:S(2)}) collective-permute-start(bf16[1056,256]{1,0:T(8,128)(2,1)S(1)} %pad_maximum_fusion), channel_id=1, source_target_pairs={{0,32},{8,40},{16,48},{24,56},{32,64},{40,72},{48,80},{56,88},{64,... | collective-permute-start | bytes 1622024 | tf_op jit(solution)/shard_map/ppermute | solution.py:322
  13.2 19.9 %collective-permute-start.10 = (bf16[1056,256]{1,0:T(8,128)(2,1)S(1)}, bf16[1056,256]{1,0:T(8,128)(2,1)S(1)}, u32[]{:S(2)}, u32[]{:S(2)}) collective-permute-start(bf16[1056,256]{1,0:T(8,128)(2,1)S(1)} %pad_maximum_fusion), channel_id=1, source_target_pairs={{0,96},{8,104},{16,112},{24,120},{32,0},{40,8},{48,16},{56,24},{64... | collective-permute-start | bytes 1622024 | tf_op jit(solution)/shard_map/ppermute | solution.py:322
  15.0 8.3 %collective-permute-start.2 = (bf16[528,256]{1,0:T(8,128)(2,1)S(1)}, bf16[528,256]{1,0:T(8,128)(2,1)S(1)}, u32[]{:S(2)}, u32[]{:S(2)}) collective-permute-start(bf16[528,256]{1,0:T(8,128)(2,1)S(1)} %collective-permute-done.1.back_ref), channel_id=1, source_target_pairs={{0,8},{8,16},{16,24},{24,0},{32,40},{40,48},{48,56},{56,32},{64,72... | collective-permute-start | bytes 811016 | tf_op jit(solution)/shard_map/ppermute | solution.py:322
  16.3 0.7 copy-start.3
  18.7 5.3 %copy-start.5 = (bf16[528,256]{1,0:T(8,128)(2,1)S(1)}, bf16[528,256]{1,0:T(8,128)(2,1)}, u32[]{:S(2)}) copy-start(bf16[528,256]{1,0:T(8,128)(2,1)} %get-tuple-element.32.own_ref) | copy-start | bytes 811012
  23.3 21.5 %collective-permute-start.5 = (bf16[528,256]{1,0:T(8,128)(2,1)S(1)}, bf16[528,256]{1,0:T(8,128)(2,1)S(1)}, u32[]{:S(2)}, u32[]{:S(2)}) collective-permute-start(bf16[528,256]{1,0:T(8,128)(2,1)S(1)} %collective-permute-done.ahead_ref.ahead0), channel_id=1, source_target_pairs={{0,96},{8,104},{16,112},{24,120},{32,0},{40,8},{48,16},{56,24},{64... | collective-permute-start | bytes 811016 | tf_op jit(solution)/shard_map/ppermute | solution.py:322
  24.1 20.8 %slice-start = ((s8[6553600]{0:T(1024)(128)(4,1)}), s8[4194304]{0:T(1024)(128)(4,1)S(1)}, s32[]{:S(2)}) async-start(s8[6553600]{0:T(1024)(128)(4,1)} %bitcast.1), calls=%async_computation | async-start | bytes 8388608
  26.5 18.4 %collective-permute-start.7 = (bf16[1056,256]{1,0:T(8,128)(2,1)S(1)}, bf16[1056,256]{1,0:T(8,128)(2,1)S(1)}, u32[]{:S(2)}, u32[]{:S(2)}) collective-permute-start(bf16[1056,256]{1,0:T(8,128)(2,1)S(1)} %collective-permute-done.6.back12), channel_id=1, source_target_pairs={{0,32},{8,40},{16,48},{24,56},{32,64},{40,72},{48,80},{56,88},{64,... | collective-permute-start | bytes 1622024 | tf_op jit(solution)/shard_map/ppermute | solution.py:322
  28.0 12.4 %collective-permute-start.9 = (bf16[528,256]{1,0:T(8,128)(2,1)S(1)}, bf16[528,256]{1,0:T(8,128)(2,1)S(1)}, u32[]{:S(2)}, u32[]{:S(2)}) collective-permute-start(bf16[528,256]{1,0:T(8,128)(2,1)S(1)} %slice.6), channel_id=1, source_target_pairs={{0,24},{8,0},{16,8},{24,16},{32,56},{40,32},{48,40},{56,48},{64,88... | collective-permute-start | bytes 811016 | tf_op jit(solution)/shard_map/ppermute | solution.py:322
  33.1 11.8 %slice-start.1 = ((s8[6553600]{0:T(1024)(128)(4,1)}), s8[2359296]{0:T(1024)(128)(4,1)S(1)}, s32[]{:S(2)}) async-start(s8[6553600]{0:T(1024)(128)(4,1)} %bitcast.1), calls=%async_computation.1 | async-start | bytes 4718592
  33.1 7.7 %collective-permute-start.11 = (bf16[528,256]{1,0:T(8,128)(2,1)S(1)}, bf16[528,256]{1,0:T(8,128)(2,1)S(1)}, u32[]{:S(2)}, u32[]{:S(2)}) collective-permute-start(bf16[528,256]{1,0:T(8,128)(2,1)S(1)} %slice.8), channel_id=1, source_target_pairs={{0,8},{8,16},{16,24},{24,0},{32,40},{40,48},{48,56},{56,32},{64,72... | collective-permute-start | bytes 811016 | tf_op jit(solution)/shard_map/ppermute | solution.py:322
  33.2 11.7 %collective-permute-start.8 = (bf16[528,256]{1,0:T(8,128)(2,1)S(1)}, bf16[528,256]{1,0:T(8,128)(2,1)S(1)}, u32[]{:S(2)}, u32[]{:S(2)}) collective-permute-start(bf16[528,256]{1,0:T(8,128)(2,1)S(1)} %collective-permute-done.2.far_ref), channel_id=1, source_target_pairs={{0,64},{8,72},{16,80},{24,88},{32,96},{40,104},{48,112},{56,120},{... | collective-permute-start | bytes 811016 | tf_op jit(solution)/shard_map/ppermute | solution.py:322
  40.8 4.1 %copy-start.4 = (f32[1,512]{1,0:T(1,128)S(1)}, f32[1,512]{1,0:T(1,128)}, u32[]{:S(2)}) copy-start(f32[1,512]{1,0:T(1,128)} %get-tuple-element.34.cum_ref) | copy-start | bytes 6148
  52.5 3.2 %collective-permute-start.15 = (bf16[512,640]{1,0:T(8,128)(2,1)S(1)}, bf16[512,640]{1,0:T(8,128)(2,1)S(1)}, u32[]{:S(2)}, u32[]{:S(2)}) collective-permute-start(bf16[512,640]{1,0:T(8,128)(2,1)S(1)} %get-tuple-element.53), channel_id=1, source_target_pairs={{0,1},{1,0},{2,3},{3,2},{4,5},{5,4},{6,7},{7,6},{8,9},{9,8},{10,11... | collective-permute-start | bytes 1966088 | tf_op jit(solution)/shard_map/ppermute | solution.py:322
  55.2 4.2 %collective-permute-start.12 = (bf16[3,512,640]{2,1,0:T(8,128)(2,1)S(1)}, bf16[3,512,640]{2,1,0:T(8,128)(2,1)S(1)}, u32[]{:S(2)}, u32[]{:S(2)}) collective-permute-start(bf16[3,512,640]{2,1,0:T(8,128)(2,1)S(1)} %shard_map.71), channel_id=1, source_target_pairs={{0,1},{1,0},{2,3},{3,2},{4,5},{5,4},{6,7},{7,6},{8,9},{9,8},{10,11... | collective-permute-start | bytes 5898248 | tf_op jit(solution)/shard_map/ppermute | solution.py:322
  56.5 10.6 %collective-permute-start.16 = (bf16[256,640]{1,0:T(8,128)(2,1)S(1)}, bf16[256,640]{1,0:T(8,128)(2,1)S(1)}, u32[]{:S(2)}, u32[]{:S(2)}) collective-permute-start(bf16[256,640]{1,0:T(8,128)(2,1)S(1)} %get-tuple-element.54), channel_id=1, source_target_pairs={{0,2},{1,3},{2,4},{3,5},{4,6},{5,7},{6,0},{7,1},{8,10},{9,11},{10,... | collective-permute-start | bytes 983048 | tf_op jit(solution)/shard_map/ppermute | solution.py:322
  57.0 11.8 %collective-permute-start.17 = (bf16[256,640]{1,0:T(8,128)(2,1)S(1)}, bf16[256,640]{1,0:T(8,128)(2,1)S(1)}, u32[]{:S(2)}, u32[]{:S(2)}) collective-permute-start(bf16[256,640]{1,0:T(8,128)(2,1)S(1)} %get-tuple-element.56), channel_id=1, source_target_pairs={{0,6},{1,7},{2,0},{3,1},{4,2},{5,3},{6,4},{7,5},{8,14},{9,15},{10,... | collective-permute-start | bytes 983048 | tf_op jit(solution)/shard_map/ppermute | solution.py:322
  61.3 12.9 %collective-permute-start.13 = (bf16[256,640]{1,0:T(8,128)(2,1)S(1)}, bf16[256,640]{1,0:T(8,128)(2,1)S(1)}, u32[]{:S(2)}, u32[]{:S(2)}) collective-permute-start(bf16[256,640]{1,0:T(8,128)(2,1)S(1)} %get-tuple-element.50), channel_id=1, source_target_pairs={{0,2},{1,3},{2,4},{3,5},{4,6},{5,7},{6,0},{7,1},{8,10},{9,11},{10,... | collective-permute-start | bytes 983048 | tf_op jit(solution)/shard_map/ppermute | solution.py:322
  62.3 13.6 %collective-permute-start.14 = (bf16[256,640]{1,0:T(8,128)(2,1)S(1)}, bf16[256,640]{1,0:T(8,128)(2,1)S(1)}, u32[]{:S(2)}, u32[]{:S(2)}) collective-permute-start(bf16[256,640]{1,0:T(8,128)(2,1)S(1)} %get-tuple-element.51), channel_id=1, source_target_pairs={{0,6},{1,7},{2,0},{3,1},{4,2},{5,3},{6,4},{7,5},{8,14},{9,15},{10,... | collective-permute-start | bytes 983048 | tf_op jit(solution)/shard_map/ppermute | solution.py:322
  69.0 11.3 %collective-permute-start.18 = (bf16[256,640]{1,0:T(8,128)(2,1)S(1)}, bf16[256,640]{1,0:T(8,128)(2,1)S(1)}, u32[]{:S(2)}, u32[]{:S(2)}) collective-permute-start(bf16[256,640]{1,0:T(8,128)(2,1)S(1)} %get-tuple-element.57), channel_id=1, source_target_pairs={{0,2},{1,3},{2,4},{3,5},{4,6},{5,7},{6,0},{7,1},{8,10},{9,11},{10,... | collective-permute-start | bytes 983048 | tf_op jit(solution)/shard_map/ppermute | solution.py:322
  69.3 12.3 %collective-permute-start.19 = (bf16[256,640]{1,0:T(8,128)(2,1)S(1)}, bf16[256,640]{1,0:T(8,128)(2,1)S(1)}, u32[]{:S(2)}, u32[]{:S(2)}) collective-permute-start(bf16[256,640]{1,0:T(8,128)(2,1)S(1)} %get-tuple-element.58), channel_id=1, source_target_pairs={{0,6},{1,7},{2,0},{3,1},{4,2},{5,3},{6,4},{7,5},{8,14},{9,15},{10,... | collective-permute-start | bytes 983048 | tf_op jit(solution)/shard_map/ppermute | solution.py:322

commit v3 on v2

--- a/solution.py
+++ b/solution.py
@@ -281,10 +281,9 @@
 
 
 def other_near_body(normed_ref, weight_ref, out_ref):
-    @pl.loop(0, 3)
+    @pl.loop(0, 2)
     def _(slot):
-        step = jnp.where(slot == 0, 1, jnp.where(slot == 1, 3, 0))
-        out_ref[slot] = product(normed_ref, weight_ref, step, 1).astype(BF)
+        out_ref[slot] = product(normed_ref, weight_ref, jnp.where(slot == 0, 1, 3), 1).astype(BF)
 
 
 def mine_far_body(normed_ref, weight_ref, other_ref, far_r, far_l):
@@ -293,14 +292,15 @@
     far_l[...] = both[SPLIT:].astype(BF)
 
 
-def mine_near_body(normed_ref, weight_ref, other_ref, near_r, near_l, hold_r, hold_l, own_ref):
+def mine_near_body(normed_ref, weight_ref, other_ref, near_r, near_l, hold_r, hold_l, own_other, own_ref):
     both = product(normed_ref, weight_ref, 1, 0) + other_ref[0].astype(F32)
     hold_r[...] = both[:SPLIT]
     near_r[...] = both[SPLIT:].astype(BF)
     both = product(normed_ref, weight_ref, 3, 0) + other_ref[1].astype(F32)
     near_l[...] = both[:SPLIT].astype(BF)
     hold_l[...] = both[SPLIT:]
-    own_ref[...] = product(normed_ref, weight_ref, 0, 0) + other_ref[2].astype(F32)
+    own_other[...] = product(normed_ref, weight_ref, 0, 1).astype(BF)
+    own_ref[...] = product(normed_ref, weight_ref, 0, 0)
 
 
 def pass_body(hold_r, far_r, hold_l, far_l, out_r, out_l):
@@ -308,9 +308,9 @@
     out_l[...] = (hold_l[...] + far_l[...].astype(F32)).astype(BF)
 
 
-def gather_body(own_ref, near_r, near_l, out_ref):
+def gather_body(own_ref, other_ref, near_r, near_l, out_ref):
     near = jnp.concatenate([near_l[...], near_r[...]], axis=0).astype(F32)
-    out_ref[...] = (own_ref[...] + near).T
+    out_ref[...] = (own_ref[...] + other_ref[...].astype(F32) + near).T
 
 
 def finish_body(own_ref, sum_r, sum_l, out_ref):
@@ -397,31 +397,33 @@
     normed, other_far = after((normed, other_far))
     other_far = send(other_far, "head", CORE)
     other_near = kernel_call(
-        other_near_body, shape((3, TOK, CHUNK), BF), 30 * chunk_flops, 2**21, in_specs=[VMEM] * 2
+        other_near_body, shape((2, TOK, CHUNK), BF), 30 * chunk_flops, 2**21, in_specs=[VMEM] * 2
     )(normed, out_weight)
     other_near = send(other_near, "head", CORE)
     far_r, far_l = kernel_call(
         mine_far_body, (long_bf, short_bf), 30 * chunk_flops, 2**20, in_specs=[VMEM] * 3
     )(normed, out_weight, other_far)
+    normed, far_r, far_l = after((normed, far_r, far_l))
     far_r = send(far_r, "head", HEAD_X[1])
     far_l = send(far_l, "head", HEAD_X[-1])
-    near_r, near_l, hold_r, hold_l, own_sum = kernel_call(
+    near_r, near_l, hold_r, hold_l, other_own, own_sum = kernel_call(
         mine_near_body,
-        (short_bf, long_bf, long_f32, short_f32, shape((TOK, CHUNK), F32)),
-        3 * chunk_flops,
+        (short_bf, long_bf, long_f32, short_f32, chunk, shape((TOK, CHUNK), F32)),
+        4 * chunk_flops,
         2**22,
         in_specs=[VMEM] * 3,
     )(normed, out_weight, other_near)
     near_r = send(near_r, "head", HEAD_X[1])
     near_l = send(near_l, "head", HEAD_X[-1])
+    other_own = send(other_own, "head", CORE)
     sum_r, sum_l = kernel_call(pass_body, (long_bf, short_bf), 2**19, 2**21, in_specs=[VMEM] * 4)(
         hold_r, far_r, hold_l, far_l
     )
     sum_r = send(sum_r, "head", HEAD_X[1])
     sum_l = send(sum_l, "head", HEAD_X[-1])
     own_sum = kernel_call(
-        gather_body, shape((CHUNK, TOK), F32), 2**20, 2**22, in_specs=[VMEM] * 3
-    )(own_sum, near_r, near_l)
+        gather_body, shape((CHUNK, TOK), F32), 2**20, 2**22, in_specs=[VMEM] * 4
+    )(own_sum, other_own, near_r, near_l)
     return kernel_call(finish_body, shape((CHUNK, TOK), BF), 2**20, 2**22, in_specs=[VMEM] * 3)(
         own_sum, sum_r, sum_l
     )

time: 82.9 us -> 82.2 us (level)
    ppermute x20 -> x21, waiting for transfers between devices: 23.9 us -> 23.2 us  [send(): return lax.ppermute(value, axis, pairs)]
    ppermute x20 -> x21, starting transfers between devices: 24.4 us -> 24.6 us  [send(): return lax.ppermute(value, axis, pairs)]
  transfers between devices with their start and end apart: 20 -> 21, of which waited for: 11 -> 10; matrix products, arithmetic and copies ran while one was open for 1% -> 1% of each run, Pallas kernels for 27% -> 27%
where the time goes in v3:
time: 82.2 us; the launch traced here: 82 us
  Pallas kernels  32.5 us (40%)
  starting transfers between devices  24.6 us (30%)
  waiting for transfers between devices  23.2 us (28%)
  local copies, waits for them, and re-layouts  1.42 us (2%)
    ppermute x21, starting transfers between devices, send(): return lax.ppermute(value, axis, pairs)  24.6 us
    ppermute x21, waiting for transfers between devices, send(): return lax.ppermute(value, axis, pairs)  23.2 us
    pallas_call x1, Pallas kernels, per_device(): kernel_call(last_body, (shape((TOK, wide), BF), chunk), 4 * block_flops,...  7.58 us
    pallas_call x1, Pallas kernels, per_device(): kernel_call(middle_body, shape((2, 2, TOK, wide), F32), 24 * block_flops,...  6.98 us
    pallas_call x1, Pallas kernels, per_device(): kernel_call(near_body, (shape((2, TOK, wide), F32), stat_shape), 2 * bloc...  4 us
    pallas_call x1, Pallas kernels, per_device(): kernel_call(first_body, shape((2, TOK, wide), F32), 2 * block_flops, 2 **...  3.36 us
    pallas_call x1, Pallas kernels, per_device(): kernel_call(mine_near_body, (short_bf, long_bf, long_f32, short_f32, chun...  2.56 us
    pallas_call x1, Pallas kernels, per_device(): kernel_call(prepare_body, (shape((PAY, 2 * HEAD_DIM), BF), shape((1, TOK)...  2.04 us
  transfers between devices with their start and end apart: 21, of which 10 were waited for; matrix products, arithmetic and copies ran while one was open for 1% of the time, Pallas kernels for 27%

profile of v3, /device:TPU:30, one launch (start us, length us, event | category | flops | bytes accessed | tf_op | source)
XLA Modules:
  0.0 82.0 jit_solution(17396694749216298063)
XLA Ops:
  0.0 2.0 %shard_map.64 = (bf16[528,256]{1,0:T(8,128)(2,1)}, f32[1,512]{1,0:T(1,128)}) custom-call(bf16[512,128]{1,0:T(8,128)(2,1)} %key_ref, bf16[512,128]{1,0:T(8,128)(2,1)} %value_ref.1, f32[1,512]{1,0:T(1,128)} %bitcast.3), custom_call_target="tpu_custom_call" | custom-call | flops 8388608 | bytes 524288 | tf_op jit(solution)/shard_map/pallas_call | solution.py:328
  2.1 2.0 %collective-permute-start.1 = (bf16[528,256]{1,0:T(8,128)(2,1)}, bf16[528,256]{1,0:T(8,128)(2,1)S(1)}, u32[]{:S(2)}, u32[]{:S(2)}) collective-permute-start(bf16[528,256]{1,0:T(8,128)(2,1)} %get-tuple-element.36.own_ref), channel_id=1, source_target_pairs={{0,8},{8,16},{16,24},{24,0},{32,40},{40,48},{48,56},{56,32},{64,72... | collective-permute-start | bytes 811016 | tf_op jit(solution)/shard_map/ppermute | solution.py:322
  4.0 2.2 %collective-permute-start.4 = (bf16[528,256]{1,0:T(8,128)(2,1)}, bf16[528,256]{1,0:T(8,128)(2,1)S(1)}, u32[]{:S(2)}, u32[]{:S(2)}) collective-permute-start(bf16[528,256]{1,0:T(8,128)(2,1)} %get-tuple-element.36.own_ref), channel_id=1, source_target_pairs={{0,24},{8,0},{16,8},{24,16},{32,56},{40,32},{48,40},{56,48},{64,88... | collective-permute-start | bytes 811016 | tf_op jit(solution)/shard_map/ppermute | solution.py:322
  6.2 0.2 collective-permute-start.3
  6.5 1.8 %collective-permute-start = (bf16[528,256]{1,0:T(8,128)(2,1)}, bf16[528,256]{1,0:T(8,128)(2,1)S(1)}, u32[]{:S(2)}, u32[]{:S(2)}) collective-permute-start(bf16[528,256]{1,0:T(8,128)(2,1)} %get-tuple-element.36.own_ref), channel_id=1, source_target_pairs={{0,96},{8,104},{16,112},{24,120},{32,0},{40,8},{48,16},{56,24},{64... | collective-permute-start | bytes 811016 | tf_op jit(solution)/shard_map/ppermute | solution.py:322
  8.3 0.7 reshape.7.gain_ref
  9.0 3.9 %collective-permute-done.1.back_ref = bf16[528,256]{1,0:T(8,128)(2,1)S(1)} collective-permute-done((bf16[528,256]{1,0:T(8,128)(2,1)}, bf16[528,256]{1,0:T(8,128)(2,1)S(1)}, u32[]{:S(2)}, u32[]{:S(2)}) %collective-permute-start.1) | collective-permute-done | bytes 270368 | tf_op jit(solution)/shard_map/ppermute | solution.py:322
  12.9 0.0 collective-permute-done.4.ahead_ref
  12.9 0.3 collective-permute-start.6
  13.2 1.8 %collective-permute-start.10 = (bf16[1056,256]{1,0:T(8,128)(2,1)S(1)}, bf16[1056,256]{1,0:T(8,128)(2,1)S(1)}, u32[]{:S(2)}, u32[]{:S(2)}) collective-permute-start(bf16[1056,256]{1,0:T(8,128)(2,1)S(1)} %pad_maximum_fusion), channel_id=1, source_target_pairs={{0,96},{8,104},{16,112},{24,120},{32,0},{40,8},{48,16},{56,24},{64... | collective-permute-start | bytes 1622024 | tf_op jit(solution)/shard_map/ppermute | solution.py:322
  15.0 1.3 %collective-permute-start.2 = (bf16[528,256]{1,0:T(8,128)(2,1)S(1)}, bf16[528,256]{1,0:T(8,128)(2,1)S(1)}, u32[]{:S(2)}, u32[]{:S(2)}) collective-permute-start(bf16[528,256]{1,0:T(8,128)(2,1)S(1)} %collective-permute-done.1.back_ref), channel_id=1, source_target_pairs={{0,8},{8,16},{16,24},{24,0},{32,40},{40,48},{48,56},{56,32},{64,72... | collective-permute-start | bytes 811016 | tf_op jit(solution)/shard_map/ppermute | solution.py:322
  16.2 0.0 copy-done.1
  16.3 0.0 copy-done.2
  16.3 0.0 copy-done
  16.3 0.7 copy-done.3
  16.9 1.8 %shard_map.65.own_ref = f32[512,640]{1,0:T(8,128)S(1)} custom-call(bf16[512,640]{1,0:T(8,128)(2,1)S(1)} %copy-done, bf16[512,128]{1,0:T(8,128)(2,1)S(1)} %copy-done.1, bf16[512,128]{1,0:T(8,128)(2,1)S(1)} %copy-done.2, f32[1,512]{1,0:T(1,128)S(1)} %copy-done.3), custom_call_target="tpu_custom_call" | custom-call | flops 5368709120 | bytes 2097152 | tf_op jit(solution)/shard_map/pallas_call | solution.py:350
  18.7 0.0 copy-start.5
  18.7 0.0 collective-permute-done.3.back_ref.back0
  18.7 0.0 collective-permute-done.ahead_ref.ahead0
  18.7 3.4 %shard_map.66.first_ref = f32[2,512,640]{2,1,0:T(8,128)S(1)} custom-call(bf16[512,640]{1,0:T(8,128)(2,1)S(1)} %copy-done, bf16[528,256]{1,0:T(8,128)(2,1)S(1)} %collective-permute-done.3.back_ref.back0, bf16[528,256]{1,0:T(8,128)(2,1)S(1)} %collective-permute-done.ahead_ref.ahead0), custom_call_target="tpu_custom_call" | custom-call | flops 1342177280 | bytes 2097152 | tf_op jit(solution)/shard_map/pallas_call | solution.py:356
  22.1 1.2 %collective-permute-done.2.far_ref = bf16[528,256]{1,0:T(8,128)(2,1)S(1)} collective-permute-done((bf16[528,256]{1,0:T(8,128)(2,1)S(1)}, bf16[528,256]{1,0:T(8,128)(2,1)S(1)}, u32[]{:S(2)}, u32[]{:S(2)}) %collective-permute-start.2) | collective-permute-done | bytes 270368 | tf_op jit(solution)/shard_map/ppermute | solution.py:322
  23.3 0.7 collective-permute-start.5
  24.1 0.0 copy-done.5
  24.1 0.3 shard_map.67
  24.4 2.1 %collective-permute-done.6.back12 = bf16[1056,256]{1,0:T(8,128)(2,1)S(1)} collective-permute-done((bf16[1056,256]{1,0:T(8,128)(2,1)S(1)}, bf16[1056,256]{1,0:T(8,128)(2,1)S(1)}, u32[]{:S(2)}, u32[]{:S(2)}) %collective-permute-start.6) | collective-permute-done | bytes 540704 | tf_op jit(solution)/shard_map/ppermute | solution.py:322
  26.5 1.6 %collective-permute-start.7 = (bf16[1056,256]{1,0:T(8,128)(2,1)S(1)}, bf16[1056,256]{1,0:T(8,128)(2,1)S(1)}, u32[]{:S(2)}, u32[]{:S(2)}) collective-permute-start(bf16[1056,256]{1,0:T(8,128)(2,1)S(1)} %collective-permute-done.6.back12), channel_id=1, source_target_pairs={{0,32},{8,40},{16,48},{24,56},{32,64},{40,72},{48,80},{56,88},{64,... | collective-permute-start | bytes 1622024 | tf_op jit(solution)/shard_map/ppermute | solution.py:322
  28.0 5.0 %collective-permute-start.9 = (bf16[528,256]{1,0:T(8,128)(2,1)S(1)}, bf16[528,256]{1,0:T(8,128)(2,1)S(1)}, u32[]{:S(2)}, u32[]{:S(2)}) collective-permute-start(bf16[528,256]{1,0:T(8,128)(2,1)S(1)} %slice.6), channel_id=1, source_target_pairs={{0,24},{8,0},{16,8},{24,16},{32,56},{40,32},{48,40},{56,48},{64,88... | collective-permute-start | bytes 811016 | tf_op jit(solution)/shard_map/ppermute | solution.py:322
  33.1 0.0 collective-permute-done.10.ahead12
  33.1 0.0 slice-start.1
  33.1 0.1 collective-permute-start.11
  33.2 0.3 collective-permute-start.8
  33.5 7.0 %shard_map.68.groups = f32[2,2,512,640]{3,2,1,0:T(8,128)S(1)} custom-call(bf16[512,640]{1,0:T(8,128)(2,1)S(1)} %copy-done, bf16[528,256]{1,0:T(8,128)(2,1)S(1)} %collective-permute-done.3.back_ref.back0, bf16[1056,256]{1,0:T(8,128)(2,1)S(1)} %collective-permute-done.6.back12, bf16[528,256]{1,0:T(8,128)(2,1)S(1)} %collective-permute-done.ahead_ref.ahead0, ...), custom_call_target="tpu_custom_call" | custom-call | flops 16106127360 | bytes 4194304 | tf_op jit(solution)/shard_map/pallas_call | solution.py:369
  40.4 0.0 collective-permute-done.9.back3
  40.5 0.4 collective-permute-done.11.ahead3
  40.8 4.0 %shard_map.69 = (f32[2,512,640]{2,1,0:T(8,128)S(1)}, f32[8,128]{1,0:T(8,128)S(1)}) custom-call(bf16[512,640]{1,0:T(8,128)(2,1)S(1)} %copy-done, bf16[528,256]{1,0:T(8,128)(2,1)S(1)} %collective-permute-done.3.back_ref.back0, bf16[1056,256]{1,0:T(8,128)(2,1)S(1)} %collective-permute-done.6.back12, bf16[528,256]{1,0:T(8,128)(2,1)S(1)} %collective-permute-done.9.back3, ...), custom_call_target="tpu_custom_call" | custom-call | flops 1342177280 | bytes 4194304 | tf_op jit(solution)/shard_map/pallas_call | solution.py:377
  44.8 0.0 collective-permute-done.5.far0
  44.9 0.0 collective-permute-done.8.far3
  44.9 0.0 collective-permute-done.7.far12
  44.9 0.0 slice-done
  44.9 7.6 %shard_map.70 = (bf16[512,640]{1,0:T(8,128)(2,1)S(1)}, bf16[512,640]{1,0:T(8,128)(2,1)S(1)}) custom-call(bf16[512,640]{1,0:T(8,128)(2,1)S(1)} %copy-done, bf16[528,256]{1,0:T(8,128)(2,1)S(1)} %collective-permute-done.5.far0, bf16[1056,256]{1,0:T(8,128)(2,1)S(1)} %collective-permute-done.7.far12, bf16[528,256]{1,0:T(8,128)(2,1)S(1)} %collective-permute-done.8.far3, ...), custom_call_target="tpu_custom_call" | custom-call | flops 2684354560 | bytes 4194304 | tf_op jit(solution)/shard_map/pallas_call | solution.py:389
  52.5 0.3 collective-permute-start.12
  52.8 1.6 %shard_map.72 = bf16[2,512,640]{2,1,0:T(8,128)(2,1)S(1)} custom-call(bf16[512,640]{1,0:T(8,128)(2,1)S(1)} %get-tuple-element.56.normed_ref, bf16[640,5120]{1,0:T(8,128)(2,1)S(1)} %bitcast.2), custom_call_target="tpu_custom_call" | custom-call | flops 12582912000 | bytes 2097152 | tf_op jit(solution)/shard_map/pallas_call | solution.py:399
  54.4 0.5 collective-permute-start.13
  54.9 0.0 collective-permute-done.12.other_ref
  54.9 0.8 shard_map.71
  55.7 0.5 collective-permute-start.17
  56.2 1.6 %collective-permute-start.18 = (bf16[256,640]{1,0:T(8,128)(2,1)S(1)}, bf16[256,640]{1,0:T(8,128)(2,1)S(1)}, u32[]{:S(2)}, u32[]{:S(2)}) collective-permute-start(bf16[256,640]{1,0:T(8,128)(2,1)S(1)} %get-tuple-element.64), channel_id=1, source_target_pairs={{0,6},{1,7},{2,0},{3,1},{4,2},{5,3},{6,4},{7,5},{8,14},{9,15},{10,... | collective-permute-start | bytes 983048 | tf_op jit(solution)/shard_map/ppermute | solution.py:322
  57.8 0.0 collective-permute-done.13.other_ref
  57.8 2.6 %shard_map.73 = (bf16[256,640]{1,0:T(8,128)(2,1)S(1)}, bf16[256,640]{1,0:T(8,128)(2,1)S(1)}, f32[256,640]{1,0:T(8,128)S(1)}, f32[256,640]{1,0:T(8,128)S(1)}, bf1...) custom-call(bf16[512,640]{1,0:T(8,128)(2,1)S(1)} %get-tuple-element.56.normed_ref, bf16[640,5120]{1,0:T(8,128)(2,1)S(1)} %bitcast.2, ...), custom_call_target="tpu_custom_call" | custom-call | flops 1677721600 | bytes 4194304 | tf_op jit(solution)/shard_map/pallas_call | solution.py:409
  60.4 0.2 collective-permute-start.14
  60.6 1.6 %collective-permute-start.15 = (bf16[256,640]{1,0:T(8,128)(2,1)S(1)}, bf16[256,640]{1,0:T(8,128)(2,1)S(1)}, u32[]{:S(2)}, u32[]{:S(2)}) collective-permute-start(bf16[256,640]{1,0:T(8,128)(2,1)S(1)} %get-tuple-element.59), channel_id=1, source_target_pairs={{0,2},{1,3},{2,4},{3,5},{4,6},{5,7},{6,0},{7,1},{8,10},{9,11},{10,... | collective-permute-start | bytes 983048 | tf_op jit(solution)/shard_map/ppermute | solution.py:322
  62.2 0.4 collective-permute-start.16
  62.6 3.7 %collective-permute-done.17.far_r = bf16[256,640]{1,0:T(8,128)(2,1)S(1)} collective-permute-done((bf16[256,640]{1,0:T(8,128)(2,1)S(1)}, bf16[256,640]{1,0:T(8,128)(2,1)S(1)}, u32[]{:S(2)}, u32[]{:S(2)}) %collective-permute-start.17) | collective-permute-done | bytes 327712 | tf_op jit(solution)/shard_map/ppermute | solution.py:322
  66.3 1.2 %collective-permute-done.18.far_l = bf16[256,640]{1,0:T(8,128)(2,1)S(1)} collective-permute-done((bf16[256,640]{1,0:T(8,128)(2,1)S(1)}, bf16[256,640]{1,0:T(8,128)(2,1)S(1)}, u32[]{:S(2)}, u32[]{:S(2)}) %collective-permute-start.18) | collective-permute-done | bytes 327712 | tf_op jit(solution)/shard_map/ppermute | solution.py:322
  67.5 0.1 shard_map.75
  67.7 0.9 %collective-permute-start.19 = (bf16[256,640]{1,0:T(8,128)(2,1)S(1)}, bf16[256,640]{1,0:T(8,128)(2,1)S(1)}, u32[]{:S(2)}, u32[]{:S(2)}) collective-permute-start(bf16[256,640]{1,0:T(8,128)(2,1)S(1)} %get-tuple-element.65), channel_id=1, source_target_pairs={{0,2},{1,3},{2,4},{3,5},{4,6},{5,7},{6,0},{7,1},{8,10},{9,11},{10,... | collective-permute-start | bytes 983048 | tf_op jit(solution)/shard_map/ppermute | solution.py:322
  68.5 1.2 %collective-permute-start.20 = (bf16[256,640]{1,0:T(8,128)(2,1)S(1)}, bf16[256,640]{1,0:T(8,128)(2,1)S(1)}, u32[]{:S(2)}, u32[]{:S(2)}) collective-permute-start(bf16[256,640]{1,0:T(8,128)(2,1)S(1)} %get-tuple-element.66), channel_id=1, source_target_pairs={{0,6},{1,7},{2,0},{3,1},{4,2},{5,3},{6,4},{7,5},{8,14},{9,15},{10,... | collective-permute-start | bytes 983048 | tf_op jit(solution)/shard_map/ppermute | solution.py:322
  69.8 3.6 %collective-permute-done.15.near_r = bf16[256,640]{1,0:T(8,128)(2,1)S(1)} collective-permute-done((bf16[256,640]{1,0:T(8,128)(2,1)S(1)}, bf16[256,640]{1,0:T(8,128)(2,1)S(1)}, u32[]{:S(2)}, u32[]{:S(2)}) %collective-permute-start.15) | collective-permute-done | bytes 327712 | tf_op jit(solution)/shard_map/ppermute | solution.py:322
  73.4 1.2 %collective-permute-done.16.near_l = bf16[256,640]{1,0:T(8,128)(2,1)S(1)} collective-permute-done((bf16[256,640]{1,0:T(8,128)(2,1)S(1)}, bf16[256,640]{1,0:T(8,128)(2,1)S(1)}, u32[]{:S(2)}, u32[]{:S(2)}) %collective-permute-start.16) | collective-permute-done | bytes 327712 | tf_op jit(solution)/shard_map/ppermute | solution.py:322
  74.6 0.0 collective-permute-done.14.other_ref
  74.6 0.4 shard_map.74.own_ref
  75.0 4.6 %collective-permute-done.19.sum_r = bf16[256,640]{1,0:T(8,128)(2,1)S(1)} collective-permute-done((bf16[256,640]{1,0:T(8,128)(2,1)S(1)}, bf16[256,640]{1,0:T(8,128)(2,1)S(1)}, u32[]{:S(2)}, u32[]{:S(2)}) %collective-permute-start.19) | collective-permute-done | bytes 327712 | tf_op jit(solution)/shard_map/ppermute | solution.py:322
  79.5 1.4 %collective-permute-done.20.sum_l = bf16[256,640]{1,0:T(8,128)(2,1)S(1)} collective-permute-done((bf16[256,640]{1,0:T(8,128)(2,1)S(1)}, bf16[256,640]{1,0:T(8,128)(2,1)S(1)}, u32[]{:S(2)}, u32[]{:S(2)}) %collective-permute-start.20) | collective-permute-done | bytes 327712 | tf_op jit(solution)/shard_map/ppermute | solution.py:322
  80.9 1.1 %shard_map.76 = bf16[640,512]{1,0:T(8,128)(2,1)} custom-call(f32[640,512]{1,0:T(8,128)S(1)} %shard_map.74.own_ref, bf16[256,640]{1,0:T(8,128)(2,1)S(1)} %collective-permute-done.19.sum_r, bf16[256,640]{1,0:T(8,128)(2,1)S(1)} %collective-permute-done.20.sum_l), custom_call_target="tpu_custom_call" | custom-call | flops 1048576 | bytes 4194304 | tf_op jit(solution)/shard_map/pallas_call | solution.py:427
  (12 shorter events, 0.1 us)
Async XLA Ops:
  0.0 16.3 %copy-start.1 = (bf16[512,128]{1,0:T(8,128)(2,1)S(1)}, bf16[512,128]{1,0:T(8,128)(2,1)}, u32[]{:S(2)}) copy-start(bf16[512,128]{1,0:T(8,128)(2,1)} %key_ref) | copy-start | bytes 393220
  0.0 16.3 %copy-start.2 = (bf16[512,128]{1,0:T(8,128)(2,1)S(1)}, bf16[512,128]{1,0:T(8,128)(2,1)}, u32[]{:S(2)}) copy-start(bf16[512,128]{1,0:T(8,128)(2,1)} %value_ref.1) | copy-start | bytes 393220
  0.0 16.3 %copy-start = (bf16[512,640]{1,0:T(8,128)(2,1)S(1)}, bf16[512,640]{1,0:T(8,128)(2,1)}, u32[]{:S(2)}) copy-start(bf16[512,640]{1,0:T(8,128)(2,1)} %query_ref.11) | copy-start | bytes 1966084
  2.1 10.8 %collective-permute-start.1 = (bf16[528,256]{1,0:T(8,128)(2,1)}, bf16[528,256]{1,0:T(8,128)(2,1)S(1)}, u32[]{:S(2)}, u32[]{:S(2)}) collective-permute-start(bf16[528,256]{1,0:T(8,128)(2,1)} %get-tuple-element.36.own_ref), channel_id=1, source_target_pairs={{0,8},{8,16},{16,24},{24,0},{32,40},{40,48},{48,56},{56,32},{64,72... | collective-permute-start | bytes 811016 | tf_op jit(solution)/shard_map/ppermute | solution.py:322
  4.0 8.8 %collective-permute-start.4 = (bf16[528,256]{1,0:T(8,128)(2,1)}, bf16[528,256]{1,0:T(8,128)(2,1)S(1)}, u32[]{:S(2)}, u32[]{:S(2)}) collective-permute-start(bf16[528,256]{1,0:T(8,128)(2,1)} %get-tuple-element.36.own_ref), channel_id=1, source_target_pairs={{0,24},{8,0},{16,8},{24,16},{32,56},{40,32},{48,40},{56,48},{64,88... | collective-permute-start | bytes 811016 | tf_op jit(solution)/shard_map/ppermute | solution.py:322
  6.2 12.5 %collective-permute-start.3 = (bf16[528,256]{1,0:T(8,128)(2,1)}, bf16[528,256]{1,0:T(8,128)(2,1)S(1)}, u32[]{:S(2)}, u32[]{:S(2)}) collective-permute-start(bf16[528,256]{1,0:T(8,128)(2,1)} %get-tuple-element.36.own_ref), channel_id=1, source_target_pairs={{0,32},{8,40},{16,48},{24,56},{32,64},{40,72},{48,80},{56,88},{64,... | collective-permute-start | bytes 811016 | tf_op jit(solution)/shard_map/ppermute | solution.py:322
  6.5 12.3 %collective-permute-start = (bf16[528,256]{1,0:T(8,128)(2,1)}, bf16[528,256]{1,0:T(8,128)(2,1)S(1)}, u32[]{:S(2)}, u32[]{:S(2)}) collective-permute-start(bf16[528,256]{1,0:T(8,128)(2,1)} %get-tuple-element.36.own_ref), channel_id=1, source_target_pairs={{0,96},{8,104},{16,112},{24,120},{32,0},{40,8},{48,16},{56,24},{64... | collective-permute-start | bytes 811016 | tf_op jit(solution)/shard_map/ppermute | solution.py:322
  12.9 13.5 %collective-permute-start.6 = (bf16[1056,256]{1,0:T(8,128)(2,1)S(1)}, bf16[1056,256]{1,0:T(8,128)(2,1)S(1)}, u32[]{:S(2)}, u32[]{:S(2)}) collective-permute-start(bf16[1056,256]{1,0:T(8,128)(2,1)S(1)} %pad_maximum_fusion), channel_id=1, source_target_pairs={{0,32},{8,40},{16,48},{24,56},{32,64},{40,72},{48,80},{56,88},{64,... | collective-permute-start | bytes 1622024 | tf_op jit(solution)/shard_map/ppermute | solution.py:322
  13.2 19.9 %collective-permute-start.10 = (bf16[1056,256]{1,0:T(8,128)(2,1)S(1)}, bf16[1056,256]{1,0:T(8,128)(2,1)S(1)}, u32[]{:S(2)}, u32[]{:S(2)}) collective-permute-start(bf16[1056,256]{1,0:T(8,128)(2,1)S(1)} %pad_maximum_fusion), channel_id=1, source_target_pairs={{0,96},{8,104},{16,112},{24,120},{32,0},{40,8},{48,16},{56,24},{64... | collective-permute-start | bytes 1622024 | tf_op jit(solution)/shard_map/ppermute | solution.py:322
  15.0 8.3 %collective-permute-start.2 = (bf16[528,256]{1,0:T(8,128)(2,1)S(1)}, bf16[528,256]{1,0:T(8,128)(2,1)S(1)}, u32[]{:S(2)}, u32[]{:S(2)}) collective-permute-start(bf16[528,256]{1,0:T(8,128)(2,1)S(1)} %collective-permute-done.1.back_ref), channel_id=1, source_target_pairs={{0,8},{8,16},{16,24},{24,0},{32,40},{40,48},{48,56},{56,32},{64,72... | collective-permute-start | bytes 811016 | tf_op jit(solution)/shard_map/ppermute | solution.py:322
  16.3 0.7 copy-start.3
  18.7 5.3 %copy-start.5 = (bf16[528,256]{1,0:T(8,128)(2,1)S(1)}, bf16[528,256]{1,0:T(8,128)(2,1)}, u32[]{:S(2)}) copy-start(bf16[528,256]{1,0:T(8,128)(2,1)} %get-tuple-element.36.own_ref) | copy-start | bytes 811012
  23.3 21.5 %collective-permute-start.5 = (bf16[528,256]{1,0:T(8,128)(2,1)S(1)}, bf16[528,256]{1,0:T(8,128)(2,1)S(1)}, u32[]{:S(2)}, u32[]{:S(2)}) collective-permute-start(bf16[528,256]{1,0:T(8,128)(2,1)S(1)} %collective-permute-done.ahead_ref.ahead0), channel_id=1, source_target_pairs={{0,96},{8,104},{16,112},{24,120},{32,0},{40,8},{48,16},{56,24},{64... | collective-permute-start | bytes 811016 | tf_op jit(solution)/shard_map/ppermute | solution.py:322
  24.1 20.8 %slice-start = ((s8[6553600]{0:T(1024)(128)(4,1)}), s8[4194304]{0:T(1024)(128)(4,1)S(1)}, s32[]{:S(2)}) async-start(s8[6553600]{0:T(1024)(128)(4,1)} %bitcast.1), calls=%async_computation | async-start | bytes 8388608
  26.5 18.4 %collective-permute-start.7 = (bf16[1056,256]{1,0:T(8,128)(2,1)S(1)}, bf16[1056,256]{1,0:T(8,128)(2,1)S(1)}, u32[]{:S(2)}, u32[]{:S(2)}) collective-permute-start(bf16[1056,256]{1,0:T(8,128)(2,1)S(1)} %collective-permute-done.6.back12), channel_id=1, source_target_pairs={{0,32},{8,40},{16,48},{24,56},{32,64},{40,72},{48,80},{56,88},{64,... | collective-permute-start | bytes 1622024 | tf_op jit(solution)/shard_map/ppermute | solution.py:322
  28.0 12.4 %collective-permute-start.9 = (bf16[528,256]{1,0:T(8,128)(2,1)S(1)}, bf16[528,256]{1,0:T(8,128)(2,1)S(1)}, u32[]{:S(2)}, u32[]{:S(2)}) collective-permute-start(bf16[528,256]{1,0:T(8,128)(2,1)S(1)} %slice.6), channel_id=1, source_target_pairs={{0,24},{8,0},{16,8},{24,16},{32,56},{40,32},{48,40},{56,48},{64,88... | collective-permute-start | bytes 811016 | tf_op jit(solution)/shard_map/ppermute | solution.py:322
  33.1 11.8 %slice-start.1 = ((s8[6553600]{0:T(1024)(128)(4,1)}), s8[2359296]{0:T(1024)(128)(4,1)S(1)}, s32[]{:S(2)}) async-start(s8[6553600]{0:T(1024)(128)(4,1)} %bitcast.1), calls=%async_computation.1 | async-start | bytes 4718592
  33.1 7.7 %collective-permute-start.11 = (bf16[528,256]{1,0:T(8,128)(2,1)S(1)}, bf16[528,256]{1,0:T(8,128)(2,1)S(1)}, u32[]{:S(2)}, u32[]{:S(2)}) collective-permute-start(bf16[528,256]{1,0:T(8,128)(2,1)S(1)} %slice.8), channel_id=1, source_target_pairs={{0,8},{8,16},{16,24},{24,0},{32,40},{40,48},{48,56},{56,32},{64,72... | collective-permute-start | bytes 811016 | tf_op jit(solution)/shard_map/ppermute | solution.py:322
  33.2 11.7 %collective-permute-start.8 = (bf16[528,256]{1,0:T(8,128)(2,1)S(1)}, bf16[528,256]{1,0:T(8,128)(2,1)S(1)}, u32[]{:S(2)}, u32[]{:S(2)}) collective-permute-start(bf16[528,256]{1,0:T(8,128)(2,1)S(1)} %collective-permute-done.2.far_ref), channel_id=1, source_target_pairs={{0,64},{8,72},{16,80},{24,88},{32,96},{40,104},{48,112},{56,120},{... | collective-permute-start | bytes 811016 | tf_op jit(solution)/shard_map/ppermute | solution.py:322
  40.8 4.1 %copy-start.4 = (f32[1,512]{1,0:T(1,128)S(1)}, f32[1,512]{1,0:T(1,128)}, u32[]{:S(2)}) copy-start(f32[1,512]{1,0:T(1,128)} %get-tuple-element.38.cum_ref) | copy-start | bytes 6148
  52.5 2.4 %collective-permute-start.12 = (bf16[512,640]{1,0:T(8,128)(2,1)S(1)}, bf16[512,640]{1,0:T(8,128)(2,1)S(1)}, u32[]{:S(2)}, u32[]{:S(2)}) collective-permute-start(bf16[512,640]{1,0:T(8,128)(2,1)S(1)} %get-tuple-element.53), channel_id=1, source_target_pairs={{0,1},{1,0},{2,3},{3,2},{4,5},{5,4},{6,7},{7,6},{8,9},{9,8},{10,11... | collective-permute-start | bytes 1966088 | tf_op jit(solution)/shard_map/ppermute | solution.py:322
  54.4 3.4 %collective-permute-start.13 = (bf16[2,512,640]{2,1,0:T(8,128)(2,1)S(1)}, bf16[2,512,640]{2,1,0:T(8,128)(2,1)S(1)}, u32[]{:S(2)}, u32[]{:S(2)}) collective-permute-start(bf16[2,512,640]{2,1,0:T(8,128)(2,1)S(1)} %shard_map.72), channel_id=1, source_target_pairs={{0,1},{1,0},{2,3},{3,2},{4,5},{5,4},{6,7},{7,6},{8,9},{9,8},{10,11... | collective-permute-start | bytes 3932168 | tf_op jit(solution)/shard_map/ppermute | solution.py:322
  55.7 10.6 %collective-permute-start.17 = (bf16[256,640]{1,0:T(8,128)(2,1)S(1)}, bf16[256,640]{1,0:T(8,128)(2,1)S(1)}, u32[]{:S(2)}, u32[]{:S(2)}) collective-permute-start(bf16[256,640]{1,0:T(8,128)(2,1)S(1)} %get-tuple-element.62), channel_id=1, source_target_pairs={{0,2},{1,3},{2,4},{3,5},{4,6},{5,7},{6,0},{7,1},{8,10},{9,11},{10,... | collective-permute-start | bytes 983048 | tf_op jit(solution)/shard_map/ppermute | solution.py:322
  56.2 11.3 %collective-permute-start.18 = (bf16[256,640]{1,0:T(8,128)(2,1)S(1)}, bf16[256,640]{1,0:T(8,128)(2,1)S(1)}, u32[]{:S(2)}, u32[]{:S(2)}) collective-permute-start(bf16[256,640]{1,0:T(8,128)(2,1)S(1)} %get-tuple-element.64), channel_id=1, source_target_pairs={{0,6},{1,7},{2,0},{3,1},{4,2},{5,3},{6,4},{7,5},{8,14},{9,15},{10,... | collective-permute-start | bytes 983048 | tf_op jit(solution)/shard_map/ppermute | solution.py:322
  60.4 14.2 %collective-permute-start.14 = (bf16[512,640]{1,0:T(8,128)(2,1)S(1)}, bf16[512,640]{1,0:T(8,128)(2,1)S(1)}, u32[]{:S(2)}, u32[]{:S(2)}) collective-permute-start(bf16[512,640]{1,0:T(8,128)(2,1)S(1)} %get-tuple-element.58), channel_id=1, source_target_pairs={{0,1},{1,0},{2,3},{3,2},{4,5},{5,4},{6,7},{7,6},{8,9},{9,8},{10,11... | collective-permute-start | bytes 1966088 | tf_op jit(solution)/shard_map/ppermute | solution.py:322
  60.6 12.8 %collective-permute-start.15 = (bf16[256,640]{1,0:T(8,128)(2,1)S(1)}, bf16[256,640]{1,0:T(8,128)(2,1)S(1)}, u32[]{:S(2)}, u32[]{:S(2)}) collective-permute-start(bf16[256,640]{1,0:T(8,128)(2,1)S(1)} %get-tuple-element.59), channel_id=1, source_target_pairs={{0,2},{1,3},{2,4},{3,5},{4,6},{5,7},{6,0},{7,1},{8,10},{9,11},{10,... | collective-permute-start | bytes 983048 | tf_op jit(solution)/shard_map/ppermute | solution.py:322
  62.2 12.4 %collective-permute-start.16 = (bf16[256,640]{1,0:T(8,128)(2,1)S(1)}, bf16[256,640]{1,0:T(8,128)(2,1)S(1)}, u32[]{:S(2)}, u32[]{:S(2)}) collective-permute-start(bf16[256,640]{1,0:T(8,128)(2,1)S(1)} %get-tuple-element.60), channel_id=1, source_target_pairs={{0,6},{1,7},{2,0},{3,1},{4,2},{5,3},{6,4},{7,5},{8,14},{9,15},{10,... | collective-permute-start | bytes 983048 | tf_op jit(solution)/shard_map/ppermute | solution.py:322
  67.7 11.9 %collective-permute-start.19 = (bf16[256,640]{1,0:T(8,128)(2,1)S(1)}, bf16[256,640]{1,0:T(8,128)(2,1)S(1)}, u32[]{:S(2)}, u32[]{:S(2)}) collective-permute-start(bf16[256,640]{1,0:T(8,128)(2,1)S(1)} %get-tuple-element.65), channel_id=1, source_target_pairs={{0,2},{1,3},{2,4},{3,5},{4,6},{5,7},{6,0},{7,1},{8,10},{9,11},{10,... | collective-permute-start | bytes 983048 | tf_op jit(solution)/shard_map/ppermute | solution.py:322
  68.5 12.4 %collective-permute-start.20 = (bf16[256,640]{1,0:T(8,128)(2,1)S(1)}, bf16[256,640]{1,0:T(8,128)(2,1)S(1)}, u32[]{:S(2)}, u32[]{:S(2)}) collective-permute-start(bf16[256,640]{1,0:T(8,128)(2,1)S(1)} %get-tuple-element.66), channel_id=1, source_target_pairs={{0,6},{1,7},{2,0},{3,1},{4,2},{5,3},{6,4},{7,5},{8,14},{9,15},{10,... | collective-permute-start | bytes 983048 | tf_op jit(solution)/shard_map/ppermute | solution.py:322
